TPU v7x, 32 devices: a whole 2x2x4 slice. The times are simulated.
32 devices in a mesh: dp: 16 (over z, y, core), fsdp: 2 (over x).
Axes of the slice: x: 2, y: 2, z: 4, core: 2. Of those that a mesh axis runs over, the one named last changes fastest.
Arguments:
- acts: bfloat16 [2, 32, 512, 1024], P(None, ('dp', 'fsdp')), may hold values from -6 to 6
- cotangent: bfloat16 [2, 32, 512, 1024], P(None, ('dp', 'fsdp')), may hold values from -6 to 6
- seg_ids: int32 [2, 32, 512], P(None, ('dp', 'fsdp')), may hold values from 0 to 7, never falling along the last dimension, each value on 1 to 256 neighbouring positions
- pad_mask: int32 [2, 32, 512], P(None, ('dp', 'fsdp')), may hold values from 0 to 1, as said below
- qkv_weight: bfloat16 [1024, 3072], P('fsdp', 'dp')
- out_weight: bfloat16 [1024, 1024], P('fsdp', 'dp'), may hold values from -0.1875 to 0.1875
- in_weight: bfloat16 [1024, 4096], P('fsdp', 'dp'), may hold values from -0.1875 to 0.1875
- down_weight: bfloat16 [4096, 1024], P('fsdp', 'dp'), may hold values from -0.1875 to 0.1875
- biases: float32 [12288], replicated
- moment_first: float32 [2, 6, 32, 32], P('fsdp'), as said below
- moment_second: float32 [2, 6, 32, 32], P('fsdp'), as said below
- basis_left: float32 [2, 6, 32, 32], P('fsdp'), as said below
- basis_right: float32 [2, 6, 32, 32], P('fsdp'), as said below
- owners: int32 [12], replicated, may hold values from 0 to 1, as said below
Outputs:
- out_acts: bfloat16 [2, 32, 512, 1024], P(None, ('dp', 'fsdp'))
- in_grad: bfloat16 [2, 32, 512, 1024], P(None, ('dp', 'fsdp'))
- bias_grad: float32 [12288], replicated
- moment_first_new: float32 [2, 6, 32, 32], P('fsdp')
- moment_second_new: float32 [2, 6, 32, 32], P('fsdp')
- bias_new: float32 [12288], replicated
- bias_low: bfloat16 [12288], replicated
Inputs may be any that keep to these rules, and one draw needn't show every extreme that they name: `seg_ids`: never falling along a slot. `pad_mask`: in each slot the ones are a prefix of 384 to 512 positions and the zeros fill the rest. `owners`: every fsdp index owns at most 6 blocks and some own exactly 6. `moment_first`: slot (f, c) holds the block that owner f holds at rank c; other slots are ignored. `moment_second`: Positive; slots as in moment_first. `basis_left`: each slot is an orthogonal matrix; slots as in moment_first. `basis_right`: each slot is an orthogonal matrix; slots as in moment_first.
All inputs are finite; a program needn't handle non-finite values.
Results may differ from a plain program's by a relative error of at most 0.017.
Values may be sent and summed in bfloat16 or wider, within the bound.
A program may use at most 192 MiB of HBM per device.

v0:
```python
import functools
import math

import jax
import jax.numpy as jnp
from jax import lax
from jax.experimental import pallas as pl
from jax.experimental.pallas import tpu as pltpu
from jax.sharding import PartitionSpec as P

MESH=pl.DeviceIdType.MESH
NZ=4

def split_rows(R,L,a,b,unit=16):
    out=[];r=0
    for kind,n in (("A1",a),("A2",a),("B1",b),("B2",b)):
        if n: out.append((kind,r,n,0,L)); r+=n
    assert r==R,(r,R)
    return out
def split_lanes(R,L,a,b):
    out=[];l=0
    for kind,n in (("A1",a),("A2",a),("B1",b),("B2",b)):
        if n: out.append((kind,0,R,l,n)); l+=n
    assert l==L
    return out

EVENTS=[(dz,rx,ry) for dz in range(1-NZ,NZ) for rx in (0,1) for ry in (0,1) if (dz,rx,ry)!=(0,0,0)]
EVENTS.sort(key=lambda e:(abs(e[0])+e[1]+e[2], e[1]+e[2], -e[0]))
NEV=len(EVENTS)

def pick(i,values):
    out=jnp.int32(values[0])
    for j in range(1,len(values)):
        out=jnp.where(i==j,jnp.int32(values[j]),out)
    return out

def sends(kind,z,dz,rx,ry):
    plane=(rx==0)&(ry==0)
    turn_y=(kind[1]=="1")&(rx==1)&(ry==0)
    turn_x=(kind[1]=="2")&(rx==0)&(ry==1)
    if kind[0]=="A":
        return {"zp":plane&(dz>=0)&(z<NZ-1),"zm":plane&(dz<=0)&(z>0),"x":plane|turn_x,"y":plane|turn_y}
    return {"zp":(dz>=0)&(z<NZ-1),"zm":(dz<=0)&(z>0),"x":(dz==0)&(plane|turn_x),"y":(dz==0)&(plane|turn_y)}

WAYS=("x","y","zp","zm","s")

def region(total, N, K):
    for lanes in range(128,K+1,128):
        if total%lanes==0:
            rows=total//lanes
            if rows%16==0 and rows<=N: return rows,lanes
    raise ValueError(total)

class Gather:
    def __init__(self, mats, shards, fulls, local_sem, send_sem, recv_sem, sib_sem):
        self.mats=mats; self.sh=shards; self.full=fulls
        self.lsem,self.ssem,self.rsem,self.bsem=local_sem,send_sem,recv_sem,sib_sem
        dp=lax.axis_index("dp"); x=lax.axis_index("fsdp")
        self.dp,self.x=dp,x
        self.z=dp//4; self.y=(dp//2)%2; self.c=dp%2
        self.dev={"x":(dp,1-x),"y":(self.z*4+(1-self.y)*2+self.c,x),"zp":(dp+4,x),"zm":(dp-4,x),"s":(self.z*4+self.y*2+1-self.c,x)}
    def barrier(self):
        bar=pltpu.get_barrier_semaphore()
        for d in ("x","y","s"):
            pl.semaphore_signal(bar,inc=1,device_id=self.dev[d],device_id_type=MESH)
        @pl.when(self.z<NZ-1)
        def _(): pl.semaphore_signal(bar,inc=1,device_id=self.dev["zp"],device_id_type=MESH)
        @pl.when(self.z>0)
        def _(): pl.semaphore_signal(bar,inc=1,device_id=self.dev["zm"],device_id_type=MESH)
        inner=(self.z>0)&(self.z<NZ-1)
        @pl.when(inner)
        def _(): pl.semaphore_wait(bar,5)
        @pl.when(jnp.logical_not(inner))
        def _(): pl.semaphore_wait(bar,4)
    def place(self,m,k,dz,rx,ry):
        M=self.mats[m]; kind,r0,nr,l0,nl=M["classes"][k]
        y=self.y+ry-2*self.y*ry
        x=self.x+rx-2*self.x*rx
        src=(self.z-dz)*4+y*2+self.c
        return self.full[m].at[pl.ds(pl.multiple_of(src*M["R"]+r0,16),nr), pl.ds(pl.multiple_of(x*M["L"]+l0,128),nl)]
    def forward(self,m,k,dz,rx,ry,src):
        kind=self.mats[m]["classes"][k][0]
        dst=self.place(m,k,dz,rx,ry)
        def rel(a,b,c): return (a+NZ-1)*4+b*2+c
        child={"x":rel(dz,1,ry),"y":rel(dz,rx,1),"zp":rel(dz+1,rx,ry),"zm":rel(dz-1,rx,ry)}
        for d,cond in sends(kind,self.z,dz,rx,ry).items():
            def go(d=d):
                pltpu.make_async_remote_copy(src,dst,self.ssem.at[m,WAYS.index(d)],self.rsem.at[m,k,child[d]],
                    device_id=self.dev[d],device_id_type=MESH).start()
            if cond is True: go()
            elif cond is not False: pl.when(cond)(go)
        pltpu.make_async_remote_copy(src,dst,self.ssem.at[m,4],self.bsem.at[m,self.z-dz],device_id=self.dev["s"],device_id_type=MESH).start()
    def own(self,m):
        M=self.mats[m]
        for k,(kind,r0,nr,l0,nl) in enumerate(M["classes"]):
            self.forward(m,k,0,0,0,self.sh[m].at[pl.ds(r0,nr),pl.ds(l0,nl)])
        full=self.full[m].at[pl.ds(pl.multiple_of(self.dp*M["R"],16),M["R"]),pl.ds(pl.multiple_of(self.x*M["L"],128),M["L"])]
        pltpu.make_async_copy(self.sh[m],full,self.lsem.at[m]).start()
    def step(self,e,ms):
        dz=pick(e,[v[0] for v in EVENTS]); rx=pick(e,[v[1] for v in EVENTS]); ry=pick(e,[v[2] for v in EVENTS])
        src=self.z-dz
        @pl.when((src>=0)&(src<=NZ-1))
        def _():
            for m in ms:
                for k in range(len(self.mats[m]["classes"])):
                    ref=self.place(m,k,dz,rx,ry)
                    pltpu.make_async_copy(ref,ref,self.rsem.at[m,k,(dz+NZ-1)*4+rx*2+ry]).wait()
                    self.forward(m,k,dz,rx,ry,ref)
    def wait_bytes(self,m,total,sem):
        N,K=self.full[m].shape
        r,l=region(total,N,K)
        ref=self.full[m].at[pl.ds(0,r),pl.ds(0,l)]
        pltpu.make_async_copy(ref,ref,sem).wait()
    def own_done(self,m):
        own=self.sh[m]
        pltpu.make_async_copy(own,own,self.lsem.at[m]).wait()
    def plane_done(self,m,z0):
        N,K=self.full[m].shape
        self.wait_bytes(m,N*K//2//NZ,self.bsem.at[m,z0])
    def sends_done(self,m):
        M=self.mats[m]; N,K=self.full[m].shape
        def total(d,z):
            t=0
            for kind,r0,nr,l0,nl in M["classes"]:
                for dz,rx,ry in [(0,0,0)]+EVENTS:
                    if 0<=z-dz<=NZ-1 and sends(kind,z,dz,rx,ry)[d]: t+=nr*nl
            return t
        for d in ("x","y"):
            self.wait_bytes(m,total(d,0),self.ssem.at[m,WAYS.index(d)])
        for d in ("zp","zm"):
            for z in range(NZ):
                if total(d,z):
                    pl.when(self.z==z)(functools.partial(self.wait_bytes,m,total(d,z),self.ssem.at[m,WAYS.index(d)]))
        self.wait_bytes(m,N*K//2,self.ssem.at[m,4])
    def finish(self,m):
        self.own_done(m)
        for z in range(NZ): self.plane_done(m,z)
        self.sends_done(m)

def comm_scratch(n):
    return [pltpu.SemaphoreType.DMA((n,)),pltpu.SemaphoreType.DMA((n,5)),pltpu.SemaphoreType.DMA((n,4,8*NZ-4)),pltpu.SemaphoreType.DMA((n,NZ))] if n else []

def start_comm(mats,rest):
    n=len(mats)
    g=Gather(mats,rest[:n],rest[n:2*n],*rest[2*n:2*n+4])
    g.barrier()
    for m in range(n): g.own(m)
    return g

def gather_call(mats,shards,cid):
    n=len(mats)
    def kernel(*refs):
        g=start_comm(mats,list(refs))
        def st(e,_):
            g.step(e,range(n)); return _
        lax.fori_loop(0,NEV,st,0)
        for m in range(n): g.finish(m)
    outs=[jax.ShapeDtypeStruct((s.shape[0]*16,s.shape[1]*2),jnp.bfloat16) for s in shards]
    return pl.pallas_call(kernel,out_shape=outs,
        in_specs=[pl.BlockSpec(memory_space=pl.ANY)]*n,out_specs=[pl.BlockSpec(memory_space=pl.ANY)]*n,
        scratch_shapes=comm_scratch(n),
        compiler_params=pltpu.CompilerParams(collective_id=cid,has_side_effects=True,vmem_limit_bytes=60<<20),name="gather")(*shards)

def matdesc(beta=True):
    if beta:
        return [dict(R=192,L=512,classes=split_rows(192,512,80,16)),dict(R=64,L=512,classes=split_rows(64,512,32,0)),
            dict(R=256,L=512,classes=split_rows(256,512,96,32)),dict(R=64,L=2048,classes=split_lanes(64,2048,768,256))]
    return [dict(R=192,L=512,classes=split_rows(192,512,96,0)),dict(R=64,L=512,classes=split_rows(64,512,32,0)),
            dict(R=256,L=512,classes=split_rows(256,512,128,0)),dict(R=64,L=2048,classes=split_lanes(64,2048,1024,0))]
BF=jnp.bfloat16
F32=jnp.float32
D=1024
H=16
HD=64
FF=4096
SEQ=512
LOG2E=1.4426950408889634
VMEM_CAP=60<<20
ANY=pl.BlockSpec(memory_space=pl.ANY)
VM=pl.BlockSpec(memory_space=pltpu.VMEM)
SDS=jax.ShapeDtypeStruct
DMA=pltpu.SemaphoreType.DMA

def nn(a,b): return lax.dot_general(a,b,(((1,),(0,)),((),())),preferred_element_type=F32)
def nt(a,b): return lax.dot_general(a,b,(((1,),(1,)),((),())),preferred_element_type=F32)
def tn(a,b): return lax.dot_general(a,b,(((0,),(0,)),((),())),preferred_element_type=F32)
def part(i,n): return pl.ds(pl.multiple_of(i*n,n),n)
def loop(n,fn):
    def st(i,c):
        fn(i); return c
    lax.fori_loop(0,n,st,0)

OQ,OV,OO,O1,O2,OG1,OC1,OG2,OC2=0,D,2*D,3*D,3*D+FF,4*D+FF,5*D+FF,6*D+FF,7*D+FF

def column(row):
    return jnp.transpose(jnp.broadcast_to(row,(8,row.shape[1])))

class Quiet:
    def step(self,e,ms): pass

def comm_params(mats,cid,**kw):
    if mats: kw.update(collective_id=cid,has_side_effects=True)
    return pltpu.CompilerParams(vmem_limit_bytes=VMEM_CAP,**kw)

def full_shapes(mats,dp,fs):
    return [SDS((M["R"]*dp,M["L"]*fs),BF) for M in mats]

def attn_fwd(mats,shards,cid,x,wqkvT,bias,seg,pad,ndp,nfs):
    n=len(mats); S=x.shape[0]//SEQ; T=x.shape[0]; ms=range(n); QC=3*D//256
    def kernel(*refs):
        x_h,w_h,b_ref,seg_ref,pad_ref=refs[:5]
        sh=refs[5:5+n]; o=5+n
        qkv_o,ctxT_o,ctx_o,p_o=refs[o:o+4]
        full=refs[o+4:o+4+n]; o=o+4+n
        x_v,w_v,qkv_v,ctxT_v,ctx_v,mask_v,bc_v,pb,lsem,osem,psem=refs[o:o+11]
        sems=refs[o+11:]
        g=start_comm(mats,list(sh)+list(full)+list(sems)) if n else Quiet()
        cx=pltpu.make_async_copy(x_h,x_v,lsem.at[0]); cx.start()
        def w_load(j): return pltpu.make_async_copy(w_h.at[part(j,256)],w_v.at[part(j,256)],lsem.at[1+j])
        loop(QC,lambda j: w_load(j).start())
        bc_v[0:D,:]=column(b_ref[0:1,OQ:OQ+D])
        bc_v[D:2*D,:]=jnp.zeros((D,8),F32)
        bc_v[2*D:3*D,:]=column(b_ref[0:1,OV:OV+D])
        for s in range(S):
            seg_r=seg_ref[s:s+1,:]; pad_r=pad_ref[s:s+1,:]
            key_r=jnp.where(pad_r==1,seg_r,-1).astype(F32)
            key_c=column(key_r)[:,0:1]
            hit=(key_c==seg_r.astype(F32))|((pad_r==0)&(key_c>=0.0))
            mask_v[s]=jnp.where(hit,0.0,-1e30)
        cx.wait()
        def project(j):
            w_load(j).wait()
            r=part(j,256)
            qkv_v[r,:]=(nt(w_v[r,:],x_v[...])+bc_v[r,0:1]).astype(BF)
            pltpu.make_async_copy(qkv_v.at[r],qkv_o.at[r],osem.at[0]).start()
            g.step(j,ms)
        loop(QC,project)
        def attend(h):
            b=lax.rem(h,2)
            def p_copy(i): return pltpu.make_async_copy(pb.at[b],p_o.at[i],psem.at[b])
            @pl.when(h>=2)
            def _(): p_copy(h-2).wait()
            for s in range(S):
                cols=pl.ds(s*SEQ,SEQ)
                q=qkv_v[part(h,HD),cols]; k=qkv_v[part(h+H,HD),cols]; v=qkv_v[part(h+2*H,HD),cols]
                t=tn(k,q)*(0.125*LOG2E)+mask_v[s]
                e=jnp.exp2(t-jnp.max(t,axis=0,keepdims=True))
                p=(e*(1.0/jnp.sum(e,axis=0,keepdims=True))).astype(BF)
                pb[b,s]=p
                ctxT_v[part(h,HD),cols]=nn(v,p).astype(BF)
            p_copy(h).start()
            @pl.when(QC+h<NEV)
            def _(): g.step(QC+h,ms)
        loop(H,attend)
        ct=pltpu.make_async_copy(ctxT_v,ctxT_o,osem.at[1]); ct.start()
        def turn(i): ctx_v[:,part(i,128)]=jnp.transpose(ctxT_v[part(i,128),:])
        loop(D//128,turn)
        cc=pltpu.make_async_copy(ctx_v,ctx_o,osem.at[2]); cc.start()
        for m in ms: g.finish(m)
        pltpu.make_async_copy(qkv_v,qkv_o,osem.at[0]).wait()
        ct.wait(); cc.wait()
        for b in range(2): pltpu.make_async_copy(pb.at[b],p_o.at[b],psem.at[b]).wait()
    out=pl.pallas_call(kernel,
        out_shape=[SDS((3*D,T),BF),SDS((D,T),BF),SDS((T,D),BF),SDS((H,S,SEQ,SEQ),BF)]+full_shapes(mats,ndp,nfs),
        in_specs=[ANY,ANY,VM,VM,VM]+[ANY]*n,out_specs=[ANY]*(4+n),
        scratch_shapes=[pltpu.VMEM((T,D),BF),pltpu.VMEM((3*D,D),BF),pltpu.VMEM((3*D,T),BF),pltpu.VMEM((D,T),BF),pltpu.VMEM((T,D),BF),
            pltpu.VMEM((S,SEQ,SEQ),F32),pltpu.VMEM((3*D,8),F32),pltpu.VMEM((2,S,SEQ,SEQ),BF),DMA((1+QC,)),DMA((3,)),DMA((2,))]+comm_scratch(n),
        compiler_params=comm_params(mats,cid),name="attn_fwd")(x,wqkvT,bias,seg,pad,*shards)
    return out[:4],out[4:]

def ln(v):
    c=v-jnp.mean(v,axis=-1,keepdims=True)
    r=lax.rsqrt(jnp.mean(c*c,axis=-1,keepdims=True)+1e-12)
    return c*r,r

def feed(mats,shards,cid,x,ctx,cot,woT,wiT,wdT,bias,ndp,nfs):
    n=len(mats); T=x.shape[0]; RT=256; NT=T//RT; CH=1024; NC=FF//CH; UC=256; DC=D//4
    full_in=[] if n else [wdT]
    def kernel(*refs):
        x_h,ctx_h,cot_h,wo_h,wi_h,b_ref=refs[:6]
        o=6
        if n: sh=refs[o:o+n]; o+=n
        else: wd_h=refs[o]; o+=1
        out_o,dp1_o,dcT_o,g_ref=refs[o:o+4]; o+=4
        full=refs[o:o+n]; o+=n
        x_v,ctx_v,wo_v,won_v,wi_v,wd_v,n1_v,r1_v,hb_v,act_v,slope_v,f_v,u_v,lsem,osem=refs[o:o+15]
        sems=refs[o+15:]
        if n:
            g=start_comm(mats,list(sh)+list(full)+list(sems)); wd_h=full[0]; z=g.z
            order=[z,jnp.where(z==3,2,z+1),jnp.where(z==0,2,jnp.where(z==3,1,z-1)),jnp.where((z==0)|(z==1),3,0)]
        else:
            g=Quiet(); order=[0,1,2,3]
        def row(o,k=D): return b_ref[0:1,o:o+k]
        loads=[pltpu.make_async_copy(p,q,lsem.at[i]) for i,(p,q) in enumerate(((wo_h,wo_v),(ctx_h,ctx_v),(x_h,x_v)))]
        wl=pltpu.make_async_copy(wi_h,wi_v,lsem.at[3])
        for c in loads+[wl]: c.start()
        def wd_load(i):
            r=part(order[i],DC)
            return pltpu.make_async_copy(wd_h.at[r],wd_v.at[r],lsem.at[7+i])
        if not n:
            for i in range(4): wd_load(i).start()
        loads[0].wait()
        def turn(i): won_v[:,part(i,128)]=jnp.transpose(wo_v[part(i,128),:])
        loop(D//128,turn)
        cl=pltpu.make_async_copy(cot_h,wo_v,lsem.at[11]); cl.start()
        loads[1].wait(); loads[2].wait()
        g_ref[...]=jnp.zeros_like(g_ref)
        def join(t):
            rows=part(t,RT)
            br=nn(ctx_v[rows,:],won_v[...])+row(OO)
            nrm,r=ln(x_v[rows,:].astype(F32)+br)
            n1_v[rows,:]=nrm
            r1_v[rows,:]=jnp.broadcast_to(r,(RT,128))
            hb_v[rows,:]=(nrm*row(OG1)+row(OC1)).astype(BF)
            g.step(t,range(n))
        loop(NT,join)
        wl.wait()
        u_v[0]=nt(hb_v[...],wi_v[0:UC,:])
        def up(i):
            for b in range(2):
                ci=2*i+b
                cc=part(ci,UC)
                nx=part(lax.rem(ci+1,FF//UC),UC)
                bias_u=b_ref[0:1,part(ci+O1//UC,UC)]
                for t in range(NT):
                    rows=pl.ds(t*RT,RT)
                    u_v[1-b,rows,:]=nt(hb_v[rows,:],wi_v[nx,:])
                    u=u_v[b,rows,:]+bias_u
                    cdf=0.5+0.5*lax.erf(u*(1.0/math.sqrt(2.0)))
                    act_v[rows,cc]=(u*cdf).astype(BF)
                    slope_v[rows,cc]=(cdf+u*(jnp.exp2(u*u*(-0.5*LOG2E))*(1.0/math.sqrt(2.0*math.pi)))).astype(BF)
            g.step(NT+2*i,range(n)); g.step(NT+2*i+1,range(n))
        loop(FF//UC//2,up)
        done=NT+FF//UC
        def f_step(i,comm):
            wd_load(i).wait()
            r=part(order[i],DC)
            def tile(t):
                rows=part(t,RT)
                f_v[rows,r]=nt(act_v[rows,:],wd_v[r,:])
                if comm:
                    @pl.when(done+4*i+t<NEV)
                    def _(): g.step(done+4*i+t,range(n))
            loop(NT,tile)
        if n:
            g.own_done(0)
            for i in range(2): g.plane_done(0,order[i]); wd_load(i).start()
            for i in range(2): f_step(i,True)
            for i in range(2,4): g.plane_done(0,order[i]); wd_load(i).start()
        for i in range(2 if n else 0,4): f_step(i,False)
        cl.wait()
        cot_v=wo_v; ov=x_v; dcT_v=ctx_v
        def addg(o,v):
            for k in range(v.shape[1]//128):
                g_ref[pl.ds(o//128+k,1),:]+=v[:,k*128:(k+1)*128]
        def csum(v): return jnp.sum(v,axis=0,keepdims=True)
        def post(t):
            rows=part(t,RT)
            h1=n1_v[rows,:]*row(OG1)+row(OC1)
            n2,r2=ln(h1+(f_v[rows,:]+row(O2)))
            ov[rows,:]=(n2*row(OG2)+row(OC2)).astype(BF)
            pltpu.make_async_copy(ov.at[rows],out_o.at[rows],osem.at[0]).start()
            dy=cot_v[rows,:].astype(F32)
            addg(OG2,csum(dy*n2)); addg(OC2,csum(dy))
            e=dy*row(OG2)
            dp2=r2*(e-jnp.mean(e,axis=-1,keepdims=True)-n2*jnp.mean(e*n2,axis=-1,keepdims=True))
            dfb=dp2.astype(BF)
            hb_v[rows,:]=dfb
            addg(O2,csum(dfb.astype(F32)))
            f_v[rows,:]=dp2
            def inner(c):
                cc=part(c,CH)
                du=(nn(hb_v[rows,:],wd_v[:,cc])*slope_v[rows,cc].astype(F32)).astype(BF)
                s=csum(du.astype(F32))
                for k in range(CH//128):
                    g_ref[pl.ds(O1//128+c*(CH//128)+k,1),:]+=s[:,k*128:(k+1)*128]
                f_v[rows,:]+=nn(du,wi_v[cc,:])
            loop(NC,inner)
            dh1=f_v[rows,:]
            nrm1=n1_v[rows,:]
            addg(OG1,csum(dh1*nrm1)); addg(OC1,csum(dh1))
            e=dh1*row(OG1)
            dp1=r1_v[rows,0:1]*(e-jnp.mean(e,axis=-1,keepdims=True)-nrm1*jnp.mean(e*nrm1,axis=-1,keepdims=True))
            f_v[rows,:]=dp1
            pltpu.make_async_copy(f_v.at[rows],dp1_o.at[rows],osem.at[1]).start()
            da=dp1.astype(BF)
            addg(OO,csum(da.astype(F32)))
            hb_v[rows,:]=da
        loop(NT,post)
        def back(t):
            rows=part(t,RT)
            dcT_v[rows,:]=nt(won_v[rows,:],hb_v[...]).astype(BF)
        loop(NT,back)
        cd=pltpu.make_async_copy(dcT_v,dcT_o,osem.at[2]); cd.start()
        if n: g.sends_done(0)
        pltpu.make_async_copy(ov,out_o,osem.at[0]).wait()
        pltpu.make_async_copy(f_v,dp1_o,osem.at[1]).wait()
        cd.wait()
    V=pltpu.VMEM
    out=pl.pallas_call(kernel,
        out_shape=[SDS((T,D),BF),SDS((T,D),F32),SDS((D,T),BF),SDS((12*D//128,128),F32)]+full_shapes(mats,ndp,nfs),
        in_specs=[ANY]*5+[VM]+[ANY]*(n if n else 1),out_specs=[ANY]*3+[VM]+[ANY]*n,
        scratch_shapes=[V((T,D),BF),V((T,D),BF),V((D,D),BF),V((D,D),BF),V((FF,D),BF),V((D,FF),BF),V((T,D),F32),V((T,128),F32),
            V((T,D),BF),V((T,FF),BF),V((T,FF),BF),V((T,D),F32),V((2,T,UC),F32),DMA((12,)),DMA((3,))]+comm_scratch(n),
        compiler_params=comm_params(mats,cid),name="feed")(x,ctx,cot,woT,wiT,bias,*(shards if n else full_in))
    return out[:4]

STEP=5
decay_first=0.5
decay_second=0.5
adam_eps=1e-08
step_rate=0.4
NB=12
BS=32
LATE=2*D//128
EARLY=10*D//128
exact=lax.Precision.HIGHEST

def dot_exact(a,b,ca,cb):
    return lax.dot_general(a,b,(((ca,),(cb,)),((),())),precision=exact,preferred_element_type=F32)

class Reduce:
    def __init__(self,src,plane_buf,z_buf,ssem,psem,zsem):
        self.src,self.pb,self.zb,self.ssem,self.psem,self.zsem=src,plane_buf,z_buf,ssem,psem,zsem
        dp=lax.axis_index("dp"); self.x=lax.axis_index("fsdp")
        self.z=dp//4; self.y=(dp//2)%2; self.c=dp%2
        self.me=self.y*4+self.c*2+self.x
    def plane_peer(self,r):
        def flip(a,b): return 1-a if b else a
        return (self.z*4+flip(self.y,r&4)*2+flip(self.c,r&2),flip(self.x,r&1))
    def z_peer(self,r):
        hi,lo=self.z//2,self.z%2
        z=(1-hi if r&2 else hi)*2+(1-lo if r&1 else lo)
        return (z*4+self.y*2+self.c,self.x)
    def barrier(self):
        bar=pltpu.get_barrier_semaphore()
        for r in range(1,8): pl.semaphore_signal(bar,inc=1,device_id=self.plane_peer(r),device_id_type=MESH)
        for r in range(1,4): pl.semaphore_signal(bar,inc=1,device_id=self.z_peer(r),device_id_type=MESH)
        pl.semaphore_wait(bar,10)
    def copies(self,stage):
        buf,sem,idx=(self.pb,self.psem,self.me) if stage==0 else (self.zb,self.zsem,self.z)
        peers=[self.plane_peer(r) for r in range(1,8)] if stage==0 else [self.z_peer(r) for r in range(1,4)]
        return [pltpu.make_async_remote_copy(self.src if stage==0 else self.zb.at[idx],buf.at[idx],self.ssem.at[stage*7+i],sem.at[idx],
            device_id=p,device_id_type=MESH) for i,p in enumerate(peers)]
    def start(self):
        for c in self.copies(0): c.start()
    def gather(self,stage):
        buf,sem,idx,k=(self.pb,self.psem,self.me,8) if stage==0 else (self.zb,self.zsem,self.z,NZ)
        for q in range(k):
            @pl.when(q!=idx)
            def _(): pltpu.make_async_copy(buf.at[q],buf.at[q],sem.at[q]).wait()
    def middle(self):
        self.gather(0)
        self.pb[self.me]=self.src[...]
        tot=self.pb[0]
        for q in range(1,8): tot=tot+self.pb[q]
        self.zb[self.z]=tot
        for c in self.copies(1): c.start()
    def end(self):
        self.gather(1)
        tot=self.zb[0]
        for q in range(1,NZ): tot=tot+self.zb[q]
        return tot
    def finish(self):
        for st in (0,1):
            for c in self.copies(st): c.wait_send()

def reduce_scratch(rows):
    return [pltpu.VMEM((rows,128),F32),pltpu.VMEM((8,rows,128),F32),pltpu.VMEM((NZ,rows,128),F32),DMA((10,)),DMA((8,)),DMA((NZ,))]

def fold_tables(n):
    i=lax.broadcasted_iota(jnp.int32,(32*n,8*n),0); j=lax.broadcasted_iota(jnp.int32,(32*n,8*n),1)
    sel=jnp.where(i//4==j,1.0,0.0)
    i=lax.broadcasted_iota(jnp.int32,(32*n,128),0); j=lax.broadcasted_iota(jnp.int32,(32*n,128),1)
    mask=jnp.where(i%4==j//32,1.0,0.0)
    i=lax.broadcasted_iota(jnp.int32,(128,32),0); j=lax.broadcasted_iota(jnp.int32,(128,32),1)
    fold=jnp.where(i%32==j,1.0,0.0)
    return sel,mask,fold

def attn_tail(p,qkvT,ctxT,dcT,dp1,wqkvT,update,cid):
    S=p.shape[1]; T=S*SEQ; G=2; NI=H//G; R=G*HD; RT=256; NT=T//RT
    up=update is not None
    def kernel(*refs):
        p_h,qkv_h,c_h,d_h,dp_h,w_h=refs[:6]; o=6
        if up: g_in,b_in,mf_h,ms_h,bl_h,br_h,own_s=refs[o:o+7]; o+=7
        if up: ig_o,bg_o,mf_o,ms_o,bn_o,bl_o=refs[o:o+6]; o+=6
        else: ig_o,gl_o=refs[o:o+2]; o+=2
        pb,qkv_v,c_v,d_v,dp_v,w_v,ig_v,ones_v,psem,lsem,wsem,osem=refs[o:o+12]; o+=12
        if up:
            early_refs=refs[o:o+6]; late_refs=refs[o+6:o+12]; o+=12
            st_v,m_st,v_st,xs,xr=refs[o:o+5]; o+=5
            early=Reduce(*early_refs); late=Reduce(*late_refs); gl=late_refs[0]
        else: gl=gl_o
        def p_load(i): return pltpu.make_async_copy(p_h.at[part(i,G)],pb.at[lax.rem(i,2)],psem.at[lax.rem(i,2)])
        def chunk(i):
            out=[pltpu.make_async_copy(qkv_h.at[part(i+k*NI,R)],qkv_v.at[part(i+k*NI,R)],lsem.at[i,k]) for k in range(3)]
            return out+[pltpu.make_async_copy(a.at[part(i,R)],b.at[part(i,R)],lsem.at[i,3+k]) for k,(a,b) in enumerate(((d_h,d_v),(c_h,c_v)))]
        p_load(jnp.int32(0)).start()
        def begin(i):
            for c in chunk(i): c.start()
        loop(NI,begin)
        wl=pltpu.make_async_copy(w_h,w_v,wsem.at[0]); wl.start()
        dl=pltpu.make_async_copy(dp_h,dp_v,wsem.at[1]); dl.start()
        ones_v[...]=jnp.ones_like(ones_v)
        if up:
            early.barrier()
            early_refs[0][...]=g_in[LATE:,:]
            early.start()
            x=early.x
            states=[]
            for k,a in enumerate((mf_h,ms_h,bl_h,br_h)):
                states.append(pltpu.make_async_remote_copy(a.at[0],st_v.at[k,x],xs.at[k],xr.at[k],device_id=early.plane_peer(1),device_id_type=MESH))
                states.append(pltpu.make_async_copy(a.at[0],st_v.at[k,x],xs.at[4+k]))
            for c in states: c.start()
        def back(i):
            @pl.when(i<NI-1)
            def _(): p_load(i+1).start()
            for c in chunk(i): c.wait()
            p_load(i).wait()
            b=lax.rem(i,2)
            for s in range(S):
                cols=pl.ds(s*SEQ,SEQ)
                for h in range(G):
                    r=part(i*G+h,HD); rk=part(i*G+h+H,HD); rv=part(i*G+h+2*H,HD)
                    d=d_v[r,cols]
                    pr=pb[b,h,s]
                    q=qkv_v[r,cols]; k=qkv_v[rk,cols]; v=qkv_v[rv,cols]
                    delta=jnp.sum(d.astype(F32)*c_v[r,cols].astype(F32),axis=0,keepdims=True)
                    ds=(pr.astype(F32)*(tn(v,d)-delta)).astype(BF)
                    qkv_v[rv,cols]=nt(d,pr).astype(BF)
                    qkv_v[rk,cols]=(nt(q,ds)*0.125).astype(BF)
                    qkv_v[r,cols]=(nn(k,ds)*0.125).astype(BF)
            gl[pl.ds(i,1),:]=nt(ones_v[...],qkv_v[part(i,R),:])[0:1,:]
            gl[pl.ds(NI+i,1),:]=nt(ones_v[...],qkv_v[part(i+2*NI,R),:])[0:1,:]
            if up:
                @pl.when(i==3)
                def _(): early.middle()
        loop(NI,back)
        if up: late.start()
        wl.wait(); dl.wait()
        def finish(t):
            cols=part(t,RT)
            acc=dp_v[cols,:]
            for k in range(3):
                acc=acc+tn(qkv_v[k*D:(k+1)*D,cols],w_v[k*D:(k+1)*D,:])
            ig_v[cols,:]=acc.astype(BF)
            pltpu.make_async_copy(ig_v.at[cols],ig_o.at[cols],osem.at[0]).start()
            if up:
                @pl.when(t==1)
                def _(): late.middle()
        loop(NT,finish)
        if up:
            for c in states: c.wait()
            owner=[own_s[b] for b in range(NB)]
            rank=[]
            for b in range(NB):
                r=jnp.int32(0)
                for e in range(b): r=r+jnp.where(owner[e]==owner[b],1,0)
                rank.append(r)
            def adam(b0,n,tiles):
                sel,mask,fold=fold_tables(n)
                gs=dot_exact(dot_exact(sel,tiles,1,0)*mask,fold,1,0)
                outs=[]
                for j in range(n):
                    b=b0+j
                    at=jnp.minimum(rank[b],st_v.shape[2]-1)
                    first,second,left,right=[st_v[k,owner[b],at] for k in range(4)]
                    t=dot_exact(dot_exact(left,gs[j*BS:(j+1)*BS,:],0,0),right,1,0)
                    m=decay_first*first+(1.0-decay_first)*t
                    v=decay_second*second+(1.0-decay_second)*t*t
                    m_st[b]=m; v_st[b]=v
                    un=(m/(1.0-decay_first**STEP))/(jnp.sqrt(v/(1.0-decay_second**STEP))+adam_eps)
                    outs.append(dot_exact(dot_exact(left,un,1,0),right,1,1))
                back_=dot_exact(jnp.concatenate(outs,0),fold,1,1)*mask
                new=b_in[8*b0:8*(b0+n),:]-step_rate*dot_exact(sel,back_,0,0)
                bg_o[8*b0:8*(b0+n),:]=tiles
                bn_o[8*b0:8*(b0+n),:]=new
                bl_o[8*b0:8*(b0+n),:]=new.astype(BF)
            adam(2,10,early.end())
            adam(0,2,late.end())
            for c in range(mf_o.shape[1]):
                at=jnp.int32(0); hit=jnp.int32(0)
                for b in range(NB):
                    here=(owner[b]==x)&(rank[b]==c)
                    at=at+jnp.where(here,b,0); hit=hit+jnp.where(here,1,0)
                at=jnp.minimum(at,NB-1)
                filled=hit.astype(F32)
                mf_o[0,c]=m_st[at]*filled
                ms_o[0,c]=v_st[at]*filled
            early.finish(); late.finish()
        pltpu.make_async_copy(ig_v,ig_o,osem.at[0]).wait()
    V=pltpu.VMEM
    scr=[V((2,G,S,SEQ,SEQ),BF),V((3*D,T),BF),V((D,T),BF),V((D,T),BF),V((T,D),F32),V((3*D,D),BF),V((T,D),BF),V((8,T),BF),DMA((2,)),DMA((NI,5)),DMA((2,)),DMA((1,))]
    ins=[p,qkvT,ctxT,dcT,dp1,wqkvT]; specs=[ANY]*6
    outs=[SDS((T,D),BF)]; ospecs=[ANY]
    if up:
        g,bias,mf,ms,bl,br,owners=update
        ins+=[g,bias,mf,ms,bl,br,owners]; specs+=[VM,VM]+[ANY]*4+[pl.BlockSpec(memory_space=pltpu.SMEM)]
        outs+=[SDS((NB*8,128),F32),SDS(mf.shape,F32),SDS(mf.shape,F32),SDS((NB*8,128),F32),SDS((NB*8,128),BF)]; ospecs+=[VM]*5
        st=(4,2)+mf.shape[1:]
        scr+=reduce_scratch(EARLY)+reduce_scratch(LATE)+[V(st,F32),V((NB,BS,BS),F32),V((NB,BS,BS),F32),DMA((8,)),DMA((4,))]
    else:
        outs+=[SDS((LATE,128),F32)]; ospecs+=[VM]
    return pl.pallas_call(kernel,out_shape=outs,in_specs=specs,out_specs=ospecs,scratch_shapes=scr,
        compiler_params=comm_params([1] if up else [],cid),name="attn_tail")(*ins)


def placement_table(owners, owner_count, capacity):
    block_count = owners.shape[0]
    index_b = jnp.arange(block_count, dtype=jnp.int32)
    same_owner = owners[:, None] == owners[None, :]
    earlier = index_b[None, :] < index_b[:, None]
    rank_of = jnp.sum((same_owner & earlier).astype(jnp.int32), axis=1)
    owner_hit = owners[None, None, :] == jnp.arange(owner_count, dtype=jnp.int32)[:, None, None]
    slot_hit = rank_of[None, None, :] == jnp.arange(capacity, dtype=jnp.int32)[None, :, None]
    return (owner_hit & slot_hit).astype(jnp.float32)


def adam_rotated(grad_slots, value_slots, first_old, second_old, left_basis, right_basis, filled):
    turned = jnp.einsum("fcki,fckj->fcij", left_basis, grad_slots, precision=exact)
    turned = jnp.einsum("fcik,fckj->fcij", turned, right_basis, precision=exact)
    first_raw = decay_first * first_old + (1.0 - decay_first) * turned
    second_raw = decay_second * second_old + (1.0 - decay_second) * turned * turned
    normed_step = (
        first_raw
        / (1.0 - decay_first**STEP)
        / (jnp.sqrt(second_raw / (1.0 - decay_second**STEP)) + adam_eps)
    )
    restored = jnp.einsum("fcik,fckj->fcij", left_basis, normed_step, precision=exact)
    restored = jnp.einsum("fcik,fcjk->fcij", restored, right_basis, precision=exact)
    value_new = value_slots - step_rate * restored
    return (first_raw * filled, second_raw * filled, value_new * filled)


def body(
    acts,
    cotangent,
    seg_ids,
    pad_mask,
    qkv_weight,
    out_weight,
    in_weight,
    down_weight,
    biases,
    moment_first,
    moment_second,
    basis_left,
    basis_right,
    owners,
):
    ndp, nfs = lax.axis_size("dp"), lax.axis_size("fsdp")
    shards = [s.T for s in (qkv_weight, out_weight, in_weight, down_weight)]
    slots = acts.shape[0] * acts.shape[1]
    x = acts.reshape(slots * SEQ, D)
    cot = cotangent.reshape(slots * SEQ, D)
    seg = seg_ids.reshape(slots, SEQ)
    pad = pad_mask.reshape(slots, SEQ)
    bias = biases.reshape(1, -1)
    if (ndp, nfs) == (16, 2):
        mats = matdesc()
        (wqT,) = gather_call(mats[:1], shards[:1], 1)
        (qkvT, ctxT, ctx, p), (woT, wiT) = attn_fwd(mats[1:3], shards[1:3], 2, x, wqT, bias, seg, pad, ndp, nfs)
        out, dp1, dcT, g = feed(mats[3:], shards[3:], 3, x, ctx, cot, woT, wiT, None, bias, ndp, nfs)
        state = (g, biases.reshape(-1, 128), moment_first, moment_second, basis_left, basis_right, owners)
        ig, bg, mf, ms, bn, bl = attn_tail(p, qkvT, ctxT, dcT, dp1, wqT, state, 4)
        return (
            out.reshape(acts.shape),
            ig.reshape(acts.shape),
            bg.reshape(-1),
            mf,
            ms,
            bn.reshape(-1),
            bl.reshape(-1),
        )
    wqT, woT, wiT, wdT = [
        lax.all_gather(lax.all_gather(t, "fsdp", axis=1, tiled=True), "dp", axis=0, tiled=True) for t in shards
    ]
    (qkvT, ctxT, ctx, p), _ = attn_fwd([], [], 0, x, wqT, bias, seg, pad, ndp, nfs)
    out, dp1, dcT, g = feed([], [], 0, x, ctx, cot, woT, wiT, wdT, bias, ndp, nfs)
    ig, gl = attn_tail(p, qkvT, ctxT, dcT, dp1, wqT, None, 0)
    outputs, input_grads = out.reshape(acts.shape), ig.reshape(acts.shape)
    grad_total = jnp.concatenate([gl, g[LATE:]], 0).reshape(-1)
    block_count = owners.shape[0]
    block_side = moment_first.shape[2]
    slot_table = placement_table(owners, lax.axis_size("fsdp"), moment_first.shape[1])
    grad_slots = jnp.einsum(
        "fcb,bij->fcij",
        slot_table,
        grad_total.reshape(block_count, block_side, block_side),
        precision=exact,
    )
    summed = lax.psum(grad_slots.astype(jnp.bfloat16), "dp")
    owned_grad = lax.psum_scatter(summed, "fsdp", scatter_dimension=0, tiled=True).astype(
        jnp.float32
    )
    own_table = lax.dynamic_slice_in_dim(slot_table, lax.axis_index("fsdp"), 1, 0)
    value_slots = jnp.einsum(
        "fcb,bij->fcij",
        own_table,
        biases.reshape(block_count, block_side, block_side),
        precision=exact,
    )
    filled = jnp.sum(own_table, axis=2)[:, :, None, None]
    first_new, second_new, value_new = adam_rotated(
        owned_grad, value_slots, moment_first, moment_second, basis_left, basis_right, filled
    )
    shared_grad, shared_value = (
        lax.all_gather(owned_grad, "fsdp", axis=0, tiled=True),
        lax.all_gather(value_new, "fsdp", axis=0, tiled=True),
    )
    bias_grad = jnp.einsum("fcb,fcij->bij", slot_table, shared_grad, precision=exact).reshape(
        biases.shape[0]
    )
    bias_new = jnp.einsum("fcb,fcij->bij", slot_table, shared_value, precision=exact).reshape(
        biases.shape[0]
    )
    return (
        outputs,
        input_grads,
        bias_grad,
        first_new,
        second_new,
        bias_new,
        bias_new.astype(jnp.bfloat16),
    )


def solution(mesh):
    placed = (
        P(None, ("dp", "fsdp"), None, None),
        P(None, ("dp", "fsdp"), None, None),
        P(None, ("dp", "fsdp"), None),
        P(None, ("dp", "fsdp"), None),
        P("fsdp", "dp"),
        P("fsdp", "dp"),
        P("fsdp", "dp"),
        P("fsdp", "dp"),
        P(),
        P("fsdp", None, None, None),
        P("fsdp", None, None, None),
        P("fsdp", None, None, None),
        P("fsdp", None, None, None),
        P(),
    )
    return jax.shard_map(
        body,
        mesh=mesh,
        in_specs=placed,
        out_specs=(
            P(None, ("dp", "fsdp"), None, None),
            P(None, ("dp", "fsdp"), None, None),
            P(),
            P("fsdp", None, None, None),
            P("fsdp", None, None, None),
            P(),
            P(),
        ),
        check_vma=False,
    )
```

profile of v0, /device:TPU:0, one launch (start us, length us, event | category | flops | bytes accessed | tf_op | source)
XLA Modules:
  0.0 236.9 jit_solution(15569638315654708691)
XLA Ops:
  0.6 1.3 copy_bitcast_fusion
  1.9 1.8 copy.21
  3.7 36.3 %gather.1.refs_1_.refs_5_ = bf16[3072,1024]{1,0:T(8,128)(2,1)} custom-call(bf16[192,512]{1,0:T(8,128)(2,1)} %bitcast.31), custom_call_target="tpu_custom_call" | custom-call | tf_op jit(solution)/shard_map/gather/pallas_call | solution.py:159
  40.0 59.7 %attn_fwd.1 = (bf16[3072,1024]{1,0:T(8,128)(2,1)}, bf16[1024,1024]{1,0:T(8,128)(2,1)}, bf16[1024,1024]{1,0:T(8,128)(2,1)}, bf16[16,2,512,512]{3,2,1,0:T(8,128)(2...) custom-call(bf16[1024,1024]{1,0:T(8,128)(2,1)} %bitcast.21, bf16[3072,1024]{1,0:T(8,128)(2,1)} %gather.1.refs_1_.refs_5_, ...), custom_call_target="tpu_custom_call" | custom-call | tf_op jit(solution)/shard_map/attn_fwd/pallas_call | solution.py:263
  99.7 83.5 %feed.1 = (bf16[1024,1024]{1,0:T(8,128)(2,1)}, f32[1024,1024]{1,0:T(8,128)}, bf16[1024,1024]{1,0:T(8,128)(2,1)}, f32[96,128]{1,0:T(8,128)}, bf16[1024,4096]{1,0:T(8,128)(2,1)}) custom-call(bf16[1024,1024]{1,0:T(8,128)(2,1)} %bitcast.22, bf16[1024,1024]{1,0:T(8,128)(2,1)} %get-tuple-element.23.refs_1_, bf16[1024,1024]{1,0:T(8,128)(2,1)} %bitcast.23, ...), custom_call_target="tpu_custom_call" | custom-call | tf_op jit(solution)/shard_map/feed/pallas_call | solution.py:400
  183.2 0.0 copy-start
  183.2 46.9 %attn_tail.1 = (bf16[1024,1024]{1,0:T(8,128)(2,1)}, f32[96,128]{1,0:T(8,128)}, f32[1,6,32,32]{3,2,1,0:T(8,128)}, f32[1,6,32,32]{3,2,1,0:T(8,128)}, f32[96,128]{1,0:T(8,128)}, /*index=5*/bf16[96,128]{1,0:T(8,128)(2,1)}) custom-call(bf16[16,2,512,512]{3,2,1,0:T(8,128)(2,1)} %get-tuple-element.27.refs_0_, bf16[3072,1024]{1,0:T(8,128)(2,1)} %get-tuple-element.28.refs_1_, ...), custom_call_target="tpu_custom_call" | custom-call | tf_op jit(solution)/shard_map/attn_tail/pallas_call | solution.py:604
  230.1 0.0 copy-done
  230.1 0.0 copy-start.1
  230.1 1.3 copy.35
  231.4 1.0 copy-done.1
  232.4 0.0 copy-start.5
  232.4 0.0 copy-start.3
  232.4 0.0 copy-start.2
  232.4 0.0 copy-start.4
  232.4 0.0 copy-start.6
  232.4 1.3 copy.36
  233.8 0.0 copy-done.5
  233.8 0.6 copy.37
  234.4 0.0 copy-done.3
  234.4 0.6 copy.38
  235.0 0.0 copy-done.2
  235.0 0.6 copy.39
  235.7 0.0 copy-done.4
  235.7 0.6 copy.40
  236.3 0.0 copy-done.6
  236.3 0.6 copy.41
Async XLA Ops:
  183.2 46.9 %copy-start = (bf16[1024,1024]{1,0:T(8,128)(2,1)S(1)}, bf16[1024,1024]{1,0:T(8,128)(2,1)}, u32[]{:S(2)}) copy-start(bf16[1024,1024]{1,0:T(8,128)(2,1)} %get-tuple-element.26) | copy-start | bytes 6291460
  230.1 2.3 copy-start.1
  232.4 1.3 copy-start.5
  232.4 2.0 copy-start.3
  232.4 2.6 %copy-start.2 = (f32[1,6,32,32]{3,2,1,0:T(8,128)S(1)}, f32[1,6,32,32]{3,2,1,0:T(8,128)}, u32[]{:S(2)}) copy-start(f32[1,6,32,32]{3,2,1,0:T(8,128)} %get-tuple-element.59) | copy-start | bytes 73732
  232.4 3.3 %copy-start.4 = (f32[96,128]{1,0:T(8,128)S(1)}, f32[96,128]{1,0:T(8,128)}, u32[]{:S(2)}) copy-start(f32[96,128]{1,0:T(8,128)} %get-tuple-element.37) | copy-start | bytes 147460
  232.4 3.9 %copy-start.6 = (bf16[96,128]{1,0:T(8,128)(2,1)S(1)}, bf16[96,128]{1,0:T(8,128)(2,1)}, u32[]{:S(2)}) copy-start(bf16[96,128]{1,0:T(8,128)(2,1)} %get-tuple-element.38) | copy-start | bytes 73732
where the time goes:
time: 237 us
  Pallas kernels  226 us (95%)
  local copies, waits for them, and re-layouts  9.93 us (4%)
    pallas_call x1, Pallas kernels, feed(): pl.pallas_call(kernel, out_shape=[SDS((T, D), BF), SDS((T, D), F32), SDS(...  83.5 us
    pallas_call x1, Pallas kernels, attn_fwd(): pl.pallas_call(kernel, out_shape=[SDS((3 * D, T), BF), SDS((D, T), BF), S...  59.7 us
    pallas_call x1, Pallas kernels, attn_tail(): pl.pallas_call(kernel, out_shape=outs, in_specs=specs, out_specs=ospecs,...  46.9 us
    pallas_call x1, Pallas kernels, gather_call(): pl.pallas_call(kernel, out_shape=outs, in_specs=[pl.BlockSpec(memory_spac...  36.3 us
    unnamed x23, local copies, waits for them, and re-layouts  9.93 us

commit v1 on v0

--- a/solution.py
+++ b/solution.py
@@ -97,7 +97,8 @@
         full=self.full[m].at[pl.ds(pl.multiple_of(self.dp*M["R"],16),M["R"]),pl.ds(pl.multiple_of(self.x*M["L"],128),M["L"])]
         pltpu.make_async_copy(self.sh[m],full,self.lsem.at[m]).start()
     def step(self,e,ms):
-        dz=pick(e,[v[0] for v in EVENTS]); rx=pick(e,[v[1] for v in EVENTS]); ry=pick(e,[v[2] for v in EVENTS])
+        code=pick(e,[(v[0]+NZ-1)*4+v[1]*2+v[2] for v in EVENTS])
+        dz=code//4-(NZ-1); rx=(code//2)%2; ry=code%2
         src=self.z-dz
         @pl.when((src>=0)&(src<=NZ-1))
         def _():
@@ -140,27 +141,6 @@
 def comm_scratch(n):
     return [pltpu.SemaphoreType.DMA((n,)),pltpu.SemaphoreType.DMA((n,5)),pltpu.SemaphoreType.DMA((n,4,8*NZ-4)),pltpu.SemaphoreType.DMA((n,NZ))] if n else []
 
-def start_comm(mats,rest):
-    n=len(mats)
-    g=Gather(mats,rest[:n],rest[n:2*n],*rest[2*n:2*n+4])
-    g.barrier()
-    for m in range(n): g.own(m)
-    return g
-
-def gather_call(mats,shards,cid):
-    n=len(mats)
-    def kernel(*refs):
-        g=start_comm(mats,list(refs))
-        def st(e,_):
-            g.step(e,range(n)); return _
-        lax.fori_loop(0,NEV,st,0)
-        for m in range(n): g.finish(m)
-    outs=[jax.ShapeDtypeStruct((s.shape[0]*16,s.shape[1]*2),jnp.bfloat16) for s in shards]
-    return pl.pallas_call(kernel,out_shape=outs,
-        in_specs=[pl.BlockSpec(memory_space=pl.ANY)]*n,out_specs=[pl.BlockSpec(memory_space=pl.ANY)]*n,
-        scratch_shapes=comm_scratch(n),
-        compiler_params=pltpu.CompilerParams(collective_id=cid,has_side_effects=True,vmem_limit_bytes=60<<20),name="gather")(*shards)
-
 def matdesc(beta=True):
     if beta:
         return [dict(R=192,L=512,classes=split_rows(192,512,80,16)),dict(R=64,L=512,classes=split_rows(64,512,32,0)),
@@ -205,205 +185,231 @@
 def full_shapes(mats,dp,fs):
     return [SDS((M["R"]*dp,M["L"]*fs),BF) for M in mats]
 
-def attn_fwd(mats,shards,cid,x,wqkvT,bias,seg,pad,ndp,nfs):
-    n=len(mats); S=x.shape[0]//SEQ; T=x.shape[0]; ms=range(n); QC=3*D//256
-    def kernel(*refs):
-        x_h,w_h,b_ref,seg_ref,pad_ref=refs[:5]
-        sh=refs[5:5+n]; o=5+n
-        qkv_o,ctxT_o,ctx_o,p_o=refs[o:o+4]
-        full=refs[o+4:o+4+n]; o=o+4+n
-        x_v,w_v,qkv_v,ctxT_v,ctx_v,mask_v,bc_v,pb,lsem,osem,psem=refs[o:o+11]
-        sems=refs[o+11:]
-        g=start_comm(mats,list(sh)+list(full)+list(sems)) if n else Quiet()
-        cx=pltpu.make_async_copy(x_h,x_v,lsem.at[0]); cx.start()
-        def w_load(j): return pltpu.make_async_copy(w_h.at[part(j,256)],w_v.at[part(j,256)],lsem.at[1+j])
-        loop(QC,lambda j: w_load(j).start())
-        bc_v[0:D,:]=column(b_ref[0:1,OQ:OQ+D])
-        bc_v[D:2*D,:]=jnp.zeros((D,8),F32)
-        bc_v[2*D:3*D,:]=column(b_ref[0:1,OV:OV+D])
-        for s in range(S):
-            seg_r=seg_ref[s:s+1,:]; pad_r=pad_ref[s:s+1,:]
-            key_r=jnp.where(pad_r==1,seg_r,-1).astype(F32)
-            key_c=column(key_r)[:,0:1]
-            hit=(key_c==seg_r.astype(F32))|((pad_r==0)&(key_c>=0.0))
-            mask_v[s]=jnp.where(hit,0.0,-1e30)
-        cx.wait()
-        def project(j):
-            w_load(j).wait()
-            r=part(j,256)
-            qkv_v[r,:]=(nt(w_v[r,:],x_v[...])+bc_v[r,0:1]).astype(BF)
-            pltpu.make_async_copy(qkv_v.at[r],qkv_o.at[r],osem.at[0]).start()
-            g.step(j,ms)
-        loop(QC,project)
-        def attend(h):
-            b=lax.rem(h,2)
-            def p_copy(i): return pltpu.make_async_copy(pb.at[b],p_o.at[i],psem.at[b])
-            @pl.when(h>=2)
-            def _(): p_copy(h-2).wait()
-            for s in range(S):
-                cols=pl.ds(s*SEQ,SEQ)
-                q=qkv_v[part(h,HD),cols]; k=qkv_v[part(h+H,HD),cols]; v=qkv_v[part(h+2*H,HD),cols]
-                t=tn(k,q)*(0.125*LOG2E)+mask_v[s]
-                e=jnp.exp2(t-jnp.max(t,axis=0,keepdims=True))
-                p=(e*(1.0/jnp.sum(e,axis=0,keepdims=True))).astype(BF)
-                pb[b,s]=p
-                ctxT_v[part(h,HD),cols]=nn(v,p).astype(BF)
-            p_copy(h).start()
-            @pl.when(QC+h<NEV)
-            def _(): g.step(QC+h,ms)
-        loop(H,attend)
-        ct=pltpu.make_async_copy(ctxT_v,ctxT_o,osem.at[1]); ct.start()
-        def turn(i): ctx_v[:,part(i,128)]=jnp.transpose(ctxT_v[part(i,128),:])
-        loop(D//128,turn)
-        cc=pltpu.make_async_copy(ctx_v,ctx_o,osem.at[2]); cc.start()
-        for m in ms: g.finish(m)
-        pltpu.make_async_copy(qkv_v,qkv_o,osem.at[0]).wait()
-        ct.wait(); cc.wait()
-        for b in range(2): pltpu.make_async_copy(pb.at[b],p_o.at[b],psem.at[b]).wait()
-    out=pl.pallas_call(kernel,
-        out_shape=[SDS((3*D,T),BF),SDS((D,T),BF),SDS((T,D),BF),SDS((H,S,SEQ,SEQ),BF)]+full_shapes(mats,ndp,nfs),
-        in_specs=[ANY,ANY,VM,VM,VM]+[ANY]*n,out_specs=[ANY]*(4+n),
-        scratch_shapes=[pltpu.VMEM((T,D),BF),pltpu.VMEM((3*D,D),BF),pltpu.VMEM((3*D,T),BF),pltpu.VMEM((D,T),BF),pltpu.VMEM((T,D),BF),
-            pltpu.VMEM((S,SEQ,SEQ),F32),pltpu.VMEM((3*D,8),F32),pltpu.VMEM((2,S,SEQ,SEQ),BF),DMA((1+QC,)),DMA((3,)),DMA((2,))]+comm_scratch(n),
-        compiler_params=comm_params(mats,cid),name="attn_fwd")(x,wqkvT,bias,seg,pad,*shards)
-    return out[:4],out[4:]
-
 def ln(v):
     c=v-jnp.mean(v,axis=-1,keepdims=True)
     r=lax.rsqrt(jnp.mean(c*c,axis=-1,keepdims=True)+1e-12)
     return c*r,r
 
-def feed(mats,shards,cid,x,ctx,cot,woT,wiT,wdT,bias,ndp,nfs):
-    n=len(mats); T=x.shape[0]; RT=256; NT=T//RT; CH=1024; NC=FF//CH; UC=256; DC=D//4
-    full_in=[] if n else [wdT]
+PACE=[13, 15, 15, 30, 34, 34, 37, 37, 39, 42, 51, 53, 53, 53, 53, 58, 58, 58, 58, 60, 60, 60, 64, 64, 67, 70, 71, 73, 78, 78, 79, 84, 84, 84, 87, 90, 90, 92, 95, 99, 101, 103, 103, 103, 106, 106, 106, 108, 108, 108, 108, 108, 108, 108, 108, 108]
+OWN={1: 18, 2: 48, 3: 78}
+
+def forward(mats,sources,cid,x,cot,bias,seg,pad,ndp,nfs):
+    comm=bool(mats); n=len(mats); S=x.shape[0]//SEQ; T=x.shape[0]
+    RT=256; NT=T//RT; CH=1024; NC=FF//CH; UC=256; DC=D//4; QC=3*D//4//256
+
     def kernel(*refs):
-        x_h,ctx_h,cot_h,wo_h,wi_h,b_ref=refs[:6]
-        o=6
-        if n: sh=refs[o:o+n]; o+=n
-        else: wd_h=refs[o]; o+=1
-        out_o,dp1_o,dcT_o,g_ref=refs[o:o+4]; o+=4
-        full=refs[o:o+n]; o+=n
-        x_v,ctx_v,wo_v,won_v,wi_v,wd_v,n1_v,r1_v,hb_v,act_v,slope_v,f_v,u_v,lsem,osem=refs[o:o+15]
-        sems=refs[o+15:]
-        if n:
-            g=start_comm(mats,list(sh)+list(full)+list(sems)); wd_h=full[0]; z=g.z
+        x_h,cot_h,b_ref,seg_ref,pad_ref=refs[:5]
+        src=refs[5:9]; o=9
+        qkv_o,ctxT_o,p_o,out_o,dp1_o,dcT_o,g_ref=refs[o:o+7]; o+=7
+        if comm: wq_h=refs[o]; o+=1
+        else: wq_h=src[0]
+        x_v,ctx_v,wo_v,won_v,wi_v,wd_v,n1_v,r1_v,hb_v,act_v,slope_v,f_v,u_v,acc_v,df_v,ga_v,gb_v,lsem,wsem,psem,osem=refs[o:o+21]; o+=21
+        loads=[pltpu.make_async_copy(x_h,x_v,lsem.at[0]),pltpu.make_async_copy(cot_h,wo_v,lsem.at[1])]
+        loads[0].start()
+        if not comm:
+            whole={m:pltpu.make_async_copy(src[m],v,lsem.at[1+m]) for m,v in ((1,wo_v),(2,wi_v),(3,wd_v))}
+            for c in whole.values(): c.start()
+        if comm:
+            in_t=refs[o]; sems=refs[o+1:]
+            g=Gather(mats,(src[0],src[1],in_t,src[3]),(wq_h,wo_v,wi_v,wd_v),*sems); g.barrier(); g.own(0)
+            eye=jnp.where(lax.broadcasted_iota(jnp.int32,(256,256),0)==lax.broadcasted_iota(jnp.int32,(256,256),1),1.0,0.0).astype(BF)
+            in_t[...]=nt(eye,src[2][...]).astype(BF)
+            z=g.z
             order=[z,jnp.where(z==3,2,z+1),jnp.where(z==0,2,jnp.where(z==3,1,z-1)),jnp.where((z==0)|(z==1),3,0)]
-        else:
-            g=Quiet(); order=[0,1,2,3]
+        else: order=[0,1,2,3]
+        def steps(m,a,b):
+            def one(e,carry):
+                g.step(e,[m])
+                for k,at in OWN.items():
+                    if (at-1)//NEV==m:
+                        @pl.when(e==(at-1)%NEV)
+                        def _(): g.own(k)
+                return carry
+            lax.fori_loop(a,b,one,0)
+        def pace(op,i,count):
+            if not comm: return
+            starts=[PACE[j-1] if j else 0 for j in range(op,op+count)]; ends=PACE[op:op+count]
+            a,b=pick(i,starts),pick(i,ends)
+            for m in range(4):
+                if starts[0]<NEV*(m+1) and ends[-1]>NEV*m and starts[0]<ends[-1]:
+                    steps(m,jnp.clip(a-NEV*m,0,NEV),jnp.clip(b-NEV*m,0,NEV))
+        def plane(m,i):
+            if comm:
+                if i==0: g.own_done(m)
+                g.plane_done(m,order[i])
+            elif i==0 and m>0: whole[m].wait()
         def row(o,k=D): return b_ref[0:1,o:o+k]
-        loads=[pltpu.make_async_copy(p,q,lsem.at[i]) for i,(p,q) in enumerate(((wo_h,wo_v),(ctx_h,ctx_v),(x_h,x_v)))]
-        wl=pltpu.make_async_copy(wi_h,wi_v,lsem.at[3])
-        for c in loads+[wl]: c.start()
-        def wd_load(i):
-            r=part(order[i],DC)
-            return pltpu.make_async_copy(wd_h.at[r],wd_v.at[r],lsem.at[7+i])
-        if not n:
-            for i in range(4): wd_load(i).start()
+        n1_v[:,0:8]=column(row(OQ)); n1_v[:,128:136]=jnp.zeros((D,8),F32); n1_v[:,256:264]=column(row(OV))
+        for s in range(S):
+            seg_r=seg_ref[s]; pad_r=pad_ref[s]
+            key_r=jnp.where(pad_r==1,seg_r,-1).astype(F32)
+            key_c=column(key_r)[:,0:1]
+            hit=(key_c==seg_r.astype(F32))|((pad_r==0)&(key_c>=0.0))
+            f_v[s*SEQ:(s+1)*SEQ,0:SEQ]=jnp.where(hit,0.0,-1e30)
+        def project(i):
+            pace(QC*i,0,1); plane(0,i)
+            def load(c): return pltpu.make_async_copy(wq_h.at[part(order[i]*QC+c,256)],slope_v.at[part(c,256),2048:3072],wsem.at[c])
+            loop(QC,lambda c: load(c).start())
+            def chunk(c):
+                jj=order[i]*QC+c; j=jj//4; rows=part(jj%4,256); cols=part(j,T)
+                load(c).wait()
+                acc=nt(slope_v[part(c,256),2048:3072],x_v[...])+n1_v[rows,part(j,128)][:,0:1]
+                act_v[rows,cols]=acc.astype(BF)
+                pltpu.make_async_copy(act_v.at[rows,cols],qkv_o.at[part(jj,256)],osem.at[0]).start()
+                @pl.when(c<QC-1)
+                def _(): pace(QC*i+1,c,QC-1)
+            loop(QC,chunk)
         loads[0].wait()
-        def turn(i): won_v[:,part(i,128)]=jnp.transpose(wo_v[part(i,128),:])
+        for i in range(4): project(i)
+        AT=4*QC
+        def attend(h):
+            pace(AT,h,H)
+            b=lax.rem(h,2)
+            def p_copy(i,s): return pltpu.make_async_copy(slope_v.at[part(b,SEQ),s*SEQ:(s+1)*SEQ],p_o.at[i,s],psem.at[b,s])
+            @pl.when(h>=2)
+            def _():
+                for s in range(S): p_copy(h-2,s).wait()
+            for s in range(S):
+                def at(j): return pl.ds(j*T+s*SEQ,SEQ)
+                r=part(h,HD)
+                q=act_v[r,at(0)]; k=act_v[r,at(1)]; v=act_v[r,at(2)]
+                t=tn(k,q)*(0.125*LOG2E)+f_v[s*SEQ:(s+1)*SEQ,0:SEQ]
+                e=jnp.exp2(t-jnp.max(t,axis=0,keepdims=True))
+                p=(e*(1.0/jnp.sum(e,axis=0,keepdims=True))).astype(BF)
+                slope_v[part(b,SEQ),s*SEQ:(s+1)*SEQ]=p
+                hb_v[r,pl.ds(s*SEQ,SEQ)]=nn(v,p).astype(BF)
+                p_copy(h,s).start()
+        loop(H,attend)
+        ct=pltpu.make_async_copy(hb_v,ctxT_o,osem.at[1]); ct.start()
+        def turn(i): ctx_v[:,part(i,128)]=jnp.transpose(hb_v[part(i,128),:])
         loop(D//128,turn)
-        cl=pltpu.make_async_copy(cot_h,wo_v,lsem.at[11]); cl.start()
-        loads[1].wait(); loads[2].wait()
+        for i in range(4): plane(1,i)
+        def turn2(i): won_v[:,part(i,128)]=jnp.transpose(wo_v[part(i,128),:])
+        loop(D//128,turn2)
+        if comm: g.sends_done(1)
+        loads[1].start()
+        pltpu.make_async_copy(act_v.at[:,0:3*T],act_v.at[:,0:3*T],osem.at[0]).wait()
+        for b in range(2):
+            for s in range(S): pltpu.make_async_copy(slope_v.at[b*SEQ:(b+1)*SEQ,s*SEQ:(s+1)*SEQ],p_o.at[b,s],psem.at[b,s]).wait()
+        ct.wait()
         g_ref[...]=jnp.zeros_like(g_ref)
         def join(t):
+            pace(AT+H,t,NT)
             rows=part(t,RT)
             br=nn(ctx_v[rows,:],won_v[...])+row(OO)
             nrm,r=ln(x_v[rows,:].astype(F32)+br)
             n1_v[rows,:]=nrm
             r1_v[rows,:]=jnp.broadcast_to(r,(RT,128))
             hb_v[rows,:]=(nrm*row(OG1)+row(OC1)).astype(BF)
-            g.step(t,range(n))
         loop(NT,join)
-        wl.wait()
-        u_v[0]=nt(hb_v[...],wi_v[0:UC,:])
+        UP=AT+H+NT
         def up(i):
-            for b in range(2):
-                ci=2*i+b
-                cc=part(ci,UC)
-                nx=part(lax.rem(ci+1,FF//UC),UC)
-                bias_u=b_ref[0:1,part(ci+O1//UC,UC)]
-                for t in range(NT):
-                    rows=pl.ds(t*RT,RT)
-                    u_v[1-b,rows,:]=nt(hb_v[rows,:],wi_v[nx,:])
-                    u=u_v[b,rows,:]+bias_u
-                    cdf=0.5+0.5*lax.erf(u*(1.0/math.sqrt(2.0)))
-                    act_v[rows,cc]=(u*cdf).astype(BF)
-                    slope_v[rows,cc]=(cdf+u*(jnp.exp2(u*u*(-0.5*LOG2E))*(1.0/math.sqrt(2.0*math.pi)))).astype(BF)
-            g.step(NT+2*i,range(n)); g.step(NT+2*i+1,range(n))
-        loop(FF//UC//2,up)
-        done=NT+FF//UC
-        def f_step(i,comm):
-            wd_load(i).wait()
+            c0=order[i]*(CH//UC)
+            pace(UP+2*i,0,1); plane(2,i)
+            u_v[0]=nt(hb_v[...],wi_v[part(c0,UC),:])
+            def two(k):
+                for b in range(2):
+                    ci=c0+2*k+b
+                    cc=part(ci,UC)
+                    nx=part(jnp.minimum(ci+1,c0+CH//UC-1),UC)
+                    bias_u=b_ref[0:1,part(ci+O1//UC,UC)]
+                    for t in range(NT):
+                        rows=pl.ds(t*RT,RT)
+                        u_v[1-b,rows,:]=nt(hb_v[rows,:],wi_v[nx,:])
+                        u=u_v[b,rows,:]+bias_u
+                        cdf=0.5+0.5*lax.erf(u*(1.0/math.sqrt(2.0)))
+                        act_v[rows,cc]=(u*cdf).astype(BF)
+                        slope_v[rows,cc]=(cdf+u*(jnp.exp2(u*u*(-0.5*LOG2E))*(1.0/math.sqrt(2.0*math.pi)))).astype(BF)
+                @pl.when(k==0)
+                def _(): pace(UP+2*i+1,0,1)
+            loop(CH//UC//2,two)
+        for i in range(4): up(i)
+        DN=UP+8
+        def down(i):
+            pace(DN+NT*i,0,1); plane(3,i)
             r=part(order[i],DC)
             def tile(t):
                 rows=part(t,RT)
                 f_v[rows,r]=nt(act_v[rows,:],wd_v[r,:])
-                if comm:
-                    @pl.when(done+4*i+t<NEV)
-                    def _(): g.step(done+4*i+t,range(n))
+                @pl.when(t<NT-1)
+                def _(): pace(DN+NT*i+1,t,NT-1)
             loop(NT,tile)
-        if n:
-            g.own_done(0)
-            for i in range(2): g.plane_done(0,order[i]); wd_load(i).start()
-            for i in range(2): f_step(i,True)
-            for i in range(2,4): g.plane_done(0,order[i]); wd_load(i).start()
-        for i in range(2 if n else 0,4): f_step(i,False)
-        cl.wait()
+        for i in range(4): down(i)
+        loads[1].wait()
         cot_v=wo_v; ov=x_v; dcT_v=ctx_v
-        def addg(o,v):
-            for k in range(v.shape[1]//128):
-                g_ref[pl.ds(o//128+k,1),:]+=v[:,k*128:(k+1)*128]
-        def csum(v): return jnp.sum(v,axis=0,keepdims=True)
-        def post(t):
-            rows=part(t,RT)
+        QR=RT//4
+        ga_v[...]=jnp.zeros_like(ga_v); gb_v[...]=jnp.zeros_like(gb_v)
+        def tally(ref,i,v):
+            at=pl.ds(pl.multiple_of(i*8,8),8)
+            ref[at,:]+=jnp.sum(v.reshape(v.shape[0]//8,8,v.shape[1]),axis=0)
+        def second(t,c,p):
+            rows=pl.ds(pl.multiple_of(t*RT+c*QR,QR),QR); rb=part(c,QR)
             h1=n1_v[rows,:]*row(OG1)+row(OC1)
             n2,r2=ln(h1+(f_v[rows,:]+row(O2)))
             ov[rows,:]=(n2*row(OG2)+row(OC2)).astype(BF)
-            pltpu.make_async_copy(ov.at[rows],out_o.at[rows],osem.at[0]).start()
             dy=cot_v[rows,:].astype(F32)
-            addg(OG2,csum(dy*n2)); addg(OC2,csum(dy))
+            tally(gb_v,0,dy*n2); tally(gb_v,1,dy)
             e=dy*row(OG2)
             dp2=r2*(e-jnp.mean(e,axis=-1,keepdims=True)-n2*jnp.mean(e*n2,axis=-1,keepdims=True))
             dfb=dp2.astype(BF)
-            hb_v[rows,:]=dfb
-            addg(O2,csum(dfb.astype(F32)))
-            f_v[rows,:]=dp2
-            def inner(c):
-                cc=part(c,CH)
-                du=(nn(hb_v[rows,:],wd_v[:,cc])*slope_v[rows,cc].astype(F32)).astype(BF)
-                s=csum(du.astype(F32))
-                for k in range(CH//128):
-                    g_ref[pl.ds(O1//128+c*(CH//128)+k,1),:]+=s[:,k*128:(k+1)*128]
-                f_v[rows,:]+=nn(du,wi_v[cc,:])
-            loop(NC,inner)
-            dh1=f_v[rows,:]
+            tally(gb_v,2,dfb.astype(F32))
+            acc_v[p,rb,:]=dp2
+            df_v[p,rb,:]=dfb
+        def first(t,c,p):
+            rows=pl.ds(pl.multiple_of(t*RT+c*QR,QR),QR); rb=part(c,QR)
+            dh1=acc_v[p,rb,:]
             nrm1=n1_v[rows,:]
-            addg(OG1,csum(dh1*nrm1)); addg(OC1,csum(dh1))
+            tally(gb_v,3,dh1*nrm1); tally(gb_v,4,dh1)
             e=dh1*row(OG1)
             dp1=r1_v[rows,0:1]*(e-jnp.mean(e,axis=-1,keepdims=True)-nrm1*jnp.mean(e*nrm1,axis=-1,keepdims=True))
             f_v[rows,:]=dp1
-            pltpu.make_async_copy(f_v.at[rows],dp1_o.at[rows],osem.at[1]).start()
             da=dp1.astype(BF)
-            addg(OO,csum(da.astype(F32)))
+            tally(gb_v,5,da.astype(F32))
             hb_v[rows,:]=da
-        loop(NT,post)
-        def back(t):
-            rows=part(t,RT)
-            dcT_v[rows,:]=nt(won_v[rows,:],hb_v[...]).astype(BF)
-        loop(NT,back)
-        cd=pltpu.make_async_copy(dcT_v,dcT_o,osem.at[2]); cd.start()
-        if n: g.sends_done(0)
-        pltpu.make_async_copy(ov,out_o,osem.at[0]).wait()
-        pltpu.make_async_copy(f_v,dp1_o,osem.at[1]).wait()
+        loop(4,lambda c: second(0,c,0))
+        for t in range(NT):
+            p=t%2
+            rows=pl.ds(t*RT,RT)
+            pltpu.make_async_copy(ov.at[rows],out_o.at[rows],osem.at[2]).start()
+            def middle(c):
+                cc=part(c,CH)
+                du=(nn(df_v[p],wd_v[:,cc])*slope_v[rows,cc].astype(F32)).astype(BF)
+                if t>0: first(t-1,c,1-p)
+                if t<NT-1: second(t+1,c,1-p)
+                tally(ga_v,c,du.astype(F32))
+                acc_v[p]+=nn(du,wi_v[cc,:])
+            loop(NC,middle)
+            if t>0:
+                back=pl.ds((t-1)*RT,RT)
+                pltpu.make_async_copy(f_v.at[back],dp1_o.at[back],osem.at[3]).start()
+        def closing(c):
+            first(NT-1,c,(NT-1)%2)
+            dcT_v[part(c,RT),0:(NT-1)*RT]=nt(won_v[part(c,RT),:],hb_v[0:(NT-1)*RT,:]).astype(BF)
+        loop(4,closing)
+        pltpu.make_async_copy(f_v.at[pl.ds((NT-1)*RT,RT)],dp1_o.at[pl.ds((NT-1)*RT,RT)],osem.at[3]).start()
+        def last(c): dcT_v[part(c,RT),(NT-1)*RT:]=nt(won_v[part(c,RT),:],hb_v[(NT-1)*RT:,:]).astype(BF)
+        loop(4,last)
+        def put(o,v):
+            for k in range(v.shape[1]//128):
+                g_ref[o//128+k:o//128+k+1,:]=v[:,k*128:(k+1)*128]
+        for i,at in enumerate((OG2,OC2,O2,OG1,OC1,OO)):
+            put(at,jnp.sum(gb_v[8*i:8*i+8,:],axis=0,keepdims=True))
+        for c in range(NC): put(O1+c*CH,jnp.sum(ga_v[8*c:8*c+8,:],axis=0,keepdims=True))
+        cd=pltpu.make_async_copy(dcT_v,dcT_o,osem.at[4]); cd.start()
+        if comm:
+            for m in (0,2,3): g.sends_done(m)
+        pltpu.make_async_copy(ov,out_o,osem.at[2]).wait()
+        pltpu.make_async_copy(f_v,dp1_o,osem.at[3]).wait()
         cd.wait()
     V=pltpu.VMEM
+    scr=[V((T,D),BF),V((T,D),BF),V((D,D),BF),V((D,D),BF),V((FF,D),BF),V((D,FF),BF),V((T,D),F32),V((T,128),F32),
+        V((T,D),BF),V((T,FF),BF),V((T,FF),BF),V((T,D),F32),V((2,T,UC),F32),V((2,RT,D),F32),V((2,RT,D),BF),V((8*NC,CH),F32),V((48,D),F32),DMA((11,)),DMA((QC,)),DMA((2,S)),DMA((5,))]
+    if comm: scr+=[V((mats[2]["R"],mats[2]["L"]),BF)]+comm_scratch(n)
     out=pl.pallas_call(kernel,
-        out_shape=[SDS((T,D),BF),SDS((T,D),F32),SDS((D,T),BF),SDS((12*D//128,128),F32)]+full_shapes(mats,ndp,nfs),
-        in_specs=[ANY]*5+[VM]+[ANY]*(n if n else 1),out_specs=[ANY]*3+[VM]+[ANY]*n,
-        scratch_shapes=[V((T,D),BF),V((T,D),BF),V((D,D),BF),V((D,D),BF),V((FF,D),BF),V((D,FF),BF),V((T,D),F32),V((T,128),F32),
-            V((T,D),BF),V((T,FF),BF),V((T,FF),BF),V((T,D),F32),V((2,T,UC),F32),DMA((12,)),DMA((3,))]+comm_scratch(n),
-        compiler_params=comm_params(mats,cid),name="feed")(x,ctx,cot,woT,wiT,bias,*(shards if n else full_in))
-    return out[:4]
+        out_shape=[SDS((3*D,T),BF),SDS((D,T),BF),SDS((H,S,SEQ,SEQ),BF),SDS((T,D),BF),SDS((T,D),F32),SDS((D,T),BF),SDS((12*D//128,128),F32)]+full_shapes(mats[:1],ndp,nfs),
+        in_specs=[ANY,ANY,VM,VM,VM]+[ANY,ANY,VM if comm else ANY,ANY],out_specs=[ANY]*6+[VM]+([ANY] if comm else []),scratch_shapes=scr,
+        compiler_params=comm_params(mats,cid),name="forward")(x,cot,bias,seg,pad,*sources)
+    return out[:7],(out[7] if comm else sources[0])
 
 STEP=5
 decay_first=0.5
@@ -482,13 +488,13 @@
     up=update is not None
     def kernel(*refs):
         p_h,qkv_h,c_h,d_h,dp_h,w_h=refs[:6]; o=6
-        if up: g_in,b_in,mf_h,ms_h,bl_h,br_h,own_s=refs[o:o+7]; o+=7
-        if up: ig_o,bg_o,mf_o,ms_o,bn_o,bl_o=refs[o:o+6]; o+=6
+        if up: g_in,mf_h,ms_h,bl_h,br_h=refs[o:o+5]; o+=5
+        if up: ig_o,gs_o,st_v=refs[o:o+3]; o+=3
         else: ig_o,gl_o=refs[o:o+2]; o+=2
         pb,qkv_v,c_v,d_v,dp_v,w_v,ig_v,ones_v,psem,lsem,wsem,osem=refs[o:o+12]; o+=12
         if up:
             early_refs=refs[o:o+6]; late_refs=refs[o+6:o+12]; o+=12
-            st_v,m_st,v_st,xs,xr=refs[o:o+5]; o+=5
+            xs,xr=refs[o:o+2]; o+=2
             early=Reduce(*early_refs); late=Reduce(*late_refs); gl=late_refs[0]
         else: gl=gl_o
         def p_load(i): return pltpu.make_async_copy(p_h.at[part(i,G)],pb.at[lax.rem(i,2)],psem.at[lax.rem(i,2)])
@@ -551,42 +557,8 @@
         loop(NT,finish)
         if up:
             for c in states: c.wait()
-            owner=[own_s[b] for b in range(NB)]
-            rank=[]
-            for b in range(NB):
-                r=jnp.int32(0)
-                for e in range(b): r=r+jnp.where(owner[e]==owner[b],1,0)
-                rank.append(r)
-            def adam(b0,n,tiles):
-                sel,mask,fold=fold_tables(n)
-                gs=dot_exact(dot_exact(sel,tiles,1,0)*mask,fold,1,0)
-                outs=[]
-                for j in range(n):
-                    b=b0+j
-                    at=jnp.minimum(rank[b],st_v.shape[2]-1)
-                    first,second,left,right=[st_v[k,owner[b],at] for k in range(4)]
-                    t=dot_exact(dot_exact(left,gs[j*BS:(j+1)*BS,:],0,0),right,1,0)
-                    m=decay_first*first+(1.0-decay_first)*t
-                    v=decay_second*second+(1.0-decay_second)*t*t
-                    m_st[b]=m; v_st[b]=v
-                    un=(m/(1.0-decay_first**STEP))/(jnp.sqrt(v/(1.0-decay_second**STEP))+adam_eps)
-                    outs.append(dot_exact(dot_exact(left,un,1,0),right,1,1))
-                back_=dot_exact(jnp.concatenate(outs,0),fold,1,1)*mask
-                new=b_in[8*b0:8*(b0+n),:]-step_rate*dot_exact(sel,back_,0,0)
-                bg_o[8*b0:8*(b0+n),:]=tiles
-                bn_o[8*b0:8*(b0+n),:]=new
-                bl_o[8*b0:8*(b0+n),:]=new.astype(BF)
-            adam(2,10,early.end())
-            adam(0,2,late.end())
-            for c in range(mf_o.shape[1]):
-                at=jnp.int32(0); hit=jnp.int32(0)
-                for b in range(NB):
-                    here=(owner[b]==x)&(rank[b]==c)
-                    at=at+jnp.where(here,b,0); hit=hit+jnp.where(here,1,0)
-                at=jnp.minimum(at,NB-1)
-                filled=hit.astype(F32)
-                mf_o[0,c]=m_st[at]*filled
-                ms_o[0,c]=v_st[at]*filled
+            gs_o[LATE:,:]=early.end()
+            gs_o[0:LATE,:]=late.end()
             early.finish(); late.finish()
         pltpu.make_async_copy(ig_v,ig_o,osem.at[0]).wait()
     V=pltpu.VMEM
@@ -594,15 +566,67 @@
     ins=[p,qkvT,ctxT,dcT,dp1,wqkvT]; specs=[ANY]*6
     outs=[SDS((T,D),BF)]; ospecs=[ANY]
     if up:
-        g,bias,mf,ms,bl,br,owners=update
-        ins+=[g,bias,mf,ms,bl,br,owners]; specs+=[VM,VM]+[ANY]*4+[pl.BlockSpec(memory_space=pltpu.SMEM)]
-        outs+=[SDS((NB*8,128),F32),SDS(mf.shape,F32),SDS(mf.shape,F32),SDS((NB*8,128),F32),SDS((NB*8,128),BF)]; ospecs+=[VM]*5
-        st=(4,2)+mf.shape[1:]
-        scr+=reduce_scratch(EARLY)+reduce_scratch(LATE)+[V(st,F32),V((NB,BS,BS),F32),V((NB,BS,BS),F32),DMA((8,)),DMA((4,))]
+        g,mf,ms,bl,br=update
+        ins+=[g,mf,ms,bl,br]; specs+=[VM]+[ANY]*4
+        outs+=[SDS((NB*8,128),F32),SDS((4,2)+mf.shape[1:],F32)]; ospecs+=[VM,VM]
+        scr+=reduce_scratch(EARLY)+reduce_scratch(LATE)+[DMA((8,)),DMA((4,))]
     else:
         outs+=[SDS((LATE,128),F32)]; ospecs+=[VM]
     return pl.pallas_call(kernel,out_shape=outs,in_specs=specs,out_specs=ospecs,scratch_shapes=scr,
         compiler_params=comm_params([1] if up else [],cid),name="attn_tail")(*ins)
+
+def update_step(out,ig,grads,state,bias,owners):
+    cap=state.shape[2]; NP=4
+    def kernel(out_h,ig_h,g_in,st_v,b_in,own_s,out_o,ig_o,bg_o,mf_o,ms_o,bn_o,bl_o,m_st,v_st,v,sem):
+        rows=out.shape[0]//NP
+        def moves(down):
+            return [pltpu.make_async_copy(*((v.at[k,pl.ds(i*rows,rows)],b.at[pl.ds(i*rows,rows)]) if down else (a.at[pl.ds(i*rows,rows)],v.at[k,pl.ds(i*rows,rows)])),sem.at[down,k,i])
+                for k,(a,b) in enumerate(((out_h,out_o),(ig_h,ig_o))) for i in range(NP)]
+        for c in moves(0): c.start()
+        x=lax.axis_index("fsdp")
+        owner=[own_s[b] for b in range(NB)]
+        rank=[]
+        for b in range(NB):
+            r=jnp.int32(0)
+            for e in range(b): r=r+jnp.where(owner[e]==owner[b],1,0)
+            rank.append(r)
+        def adam(b0,n,tiles):
+            sel,mask,fold=fold_tables(n)
+            gs=dot_exact(dot_exact(sel,tiles,1,0)*mask,fold,1,0)
+            outs=[]
+            for j in range(n):
+                b=b0+j
+                at=jnp.minimum(rank[b],st_v.shape[2]-1)
+                first,second,left,right=[st_v[k,owner[b],at] for k in range(4)]
+                t=dot_exact(dot_exact(left,gs[j*BS:(j+1)*BS,:],0,0),right,1,0)
+                m=decay_first*first+(1.0-decay_first)*t
+                v=decay_second*second+(1.0-decay_second)*t*t
+                m_st[b]=m; v_st[b]=v
+                un=(m/(1.0-decay_first**STEP))/(jnp.sqrt(v/(1.0-decay_second**STEP))+adam_eps)
+                outs.append(dot_exact(dot_exact(left,un,1,0),right,1,1))
+            back_=dot_exact(jnp.concatenate(outs,0),fold,1,1)*mask
+            new=b_in[8*b0:8*(b0+n),:]-step_rate*dot_exact(sel,back_,0,0)
+            bg_o[8*b0:8*(b0+n),:]=tiles
+            bn_o[8*b0:8*(b0+n),:]=new
+            bl_o[8*b0:8*(b0+n),:]=new.astype(BF)
+        for c,d in zip(moves(0),moves(1)): c.wait(); d.start()
+        adam(0,NB,g_in[...])
+        for c in range(mf_o.shape[1]):
+            at=jnp.int32(0); hit=jnp.int32(0)
+            for b in range(NB):
+                here=(owner[b]==x)&(rank[b]==c)
+                at=at+jnp.where(here,b,0); hit=hit+jnp.where(here,1,0)
+            at=jnp.minimum(at,NB-1)
+            filled=hit.astype(F32)
+            mf_o[0,c]=m_st[at]*filled
+            ms_o[0,c]=v_st[at]*filled
+        for c in moves(1): c.wait()
+    m=SDS((1,cap,BS,BS),F32)
+    return pl.pallas_call(kernel,
+        out_shape=[SDS(out.shape,BF),SDS(ig.shape,BF),SDS((NB*8,128),F32),m,m,SDS((NB*8,128),F32),SDS((NB*8,128),BF)],
+        in_specs=[ANY,ANY,VM,VM,VM,pl.BlockSpec(memory_space=pltpu.SMEM)],out_specs=[ANY,ANY]+[VM]*5,
+        scratch_shapes=[pltpu.VMEM((NB,BS,BS),F32),pltpu.VMEM((NB,BS,BS),F32),pltpu.VMEM((2,)+out.shape,BF),DMA((2,2,NP))],
+        compiler_params=pltpu.CompilerParams(vmem_limit_bytes=VMEM_CAP),name="update")(out,ig,grads,state,bias,owners)
 
 
 def placement_table(owners, owner_count, capacity):
@@ -649,20 +673,18 @@
     owners,
 ):
     ndp, nfs = lax.axis_size("dp"), lax.axis_size("fsdp")
-    shards = [s.T for s in (qkv_weight, out_weight, in_weight, down_weight)]
+    shards = (qkv_weight.T, out_weight.T, in_weight, down_weight.T)
     slots = acts.shape[0] * acts.shape[1]
     x = acts.reshape(slots * SEQ, D)
     cot = cotangent.reshape(slots * SEQ, D)
-    seg = seg_ids.reshape(slots, SEQ)
-    pad = pad_mask.reshape(slots, SEQ)
+    seg = seg_ids.reshape(slots, 1, SEQ)
+    pad = pad_mask.reshape(slots, 1, SEQ)
     bias = biases.reshape(1, -1)
     if (ndp, nfs) == (16, 2):
-        mats = matdesc()
-        (wqT,) = gather_call(mats[:1], shards[:1], 1)
-        (qkvT, ctxT, ctx, p), (woT, wiT) = attn_fwd(mats[1:3], shards[1:3], 2, x, wqT, bias, seg, pad, ndp, nfs)
-        out, dp1, dcT, g = feed(mats[3:], shards[3:], 3, x, ctx, cot, woT, wiT, None, bias, ndp, nfs)
-        state = (g, biases.reshape(-1, 128), moment_first, moment_second, basis_left, basis_right, owners)
-        ig, bg, mf, ms, bn, bl = attn_tail(p, qkvT, ctxT, dcT, dp1, wqT, state, 4)
+        (qkvT, ctxT, p, out, dp1, dcT, g), wqT = forward(matdesc(), shards, 1, x, cot, bias, seg, pad, ndp, nfs)
+        state = (g, moment_first, moment_second, basis_left, basis_right)
+        ig, total, state = attn_tail(p, qkvT, ctxT, dcT, dp1, wqT, state, 2)
+        out, ig, bg, mf, ms, bn, bl = update_step(out, ig, total, state, biases.reshape(-1, 128), owners)
         return (
             out.reshape(acts.shape),
             ig.reshape(acts.shape),
@@ -672,11 +694,11 @@
             bn.reshape(-1),
             bl.reshape(-1),
         )
-    wqT, woT, wiT, wdT = [
-        lax.all_gather(lax.all_gather(t, "fsdp", axis=1, tiled=True), "dp", axis=0, tiled=True) for t in shards
+    whole = [
+        lax.all_gather(lax.all_gather(t, "fsdp", axis=1, tiled=True), "dp", axis=0, tiled=True)
+        for t in (shards[0], shards[1], shards[2].T, shards[3])
     ]
-    (qkvT, ctxT, ctx, p), _ = attn_fwd([], [], 0, x, wqT, bias, seg, pad, ndp, nfs)
-    out, dp1, dcT, g = feed([], [], 0, x, ctx, cot, woT, wiT, wdT, bias, ndp, nfs)
+    (qkvT, ctxT, p, out, dp1, dcT, g), wqT = forward([], whole, 0, x, cot, bias, seg, pad, ndp, nfs)
     ig, gl = attn_tail(p, qkvT, ctxT, dcT, dp1, wqT, None, 0)
     outputs, input_grads = out.reshape(acts.shape), ig.reshape(acts.shape)
     grad_total = jnp.concatenate([gl, g[LATE:]], 0).reshape(-1)

time: 237 us -> 211 us (0.89)
  Pallas kernels: 226 us -> 210 us
  local copies, waits for them, and re-layouts: 9.93 us -> 0 us
    pallas_call x3 -> x2, Pallas kernels: 179 us -> 169 us  [the longest x1 158 us: forward(): pl.pallas_call(kernel, out_shape=[SDS((3 * D, T), BF), SDS((D, T), BF), S...]
    unnamed x23 -> x0, local copies, waits for them, and re-layouts: 9.93 us -> none
    pallas_call x1, Pallas kernels: 46.9 us -> 40.2 us  [attn_tail(): pl.pallas_call(kernel, out_shape=outs, in_specs=specs, out_specs=ospecs,...]
where the time goes in v1:
time: 211 us; the launch traced here: 210 us
  Pallas kernels  210 us (100%)
    pallas_call x1, Pallas kernels, forward(): pl.pallas_call(kernel, out_shape=[SDS((3 * D, T), BF), SDS((D, T), BF), S...  158 us
    pallas_call x1, Pallas kernels, attn_tail(): pl.pallas_call(kernel, out_shape=outs, in_specs=specs, out_specs=ospecs,...  40.2 us
    pallas_call x1, Pallas kernels, update_step(): pl.pallas_call(kernel, out_shape=[SDS(out.shape, BF), SDS(ig.shape, BF),...  10.9 us

profile of v1, /device:TPU:0, one launch (start us, length us, event | category | flops | bytes accessed | tf_op | source)
XLA Modules:
  0.0 210.4 jit_solution(3899134051481950745)
XLA Ops:
  0.6 158.4 %forward.1 = (bf16[3072,1024]{1,0:T(8,128)(2,1)}, bf16[1024,1024]{1,0:T(8,128)(2,1)}, bf16[16,2,512,512]{3,2,1,0:T(8,128)(2,1)}, bf16[1024,1024]{1,0:T(8,128)(2,...) custom-call(bf16[1024,1024]{1,0:T(8,128)(2,1)} %bitcast.16, ...), custom_call_target="tpu_custom_call" | custom-call | tf_op jit(solution)/shard_map/forward/pallas_call | solution.py:408
  159.0 40.2 %attn_tail.1 = (bf16[1024,1024]{1,0:T(8,128)(2,1)}, f32[96,128]{1,0:T(8,128)}, f32[4,2,6,32,32]{4,3,2,1,0:T(8,128)}) custom-call(bf16[16,2,512,512]{3,2,1,0:T(8,128)(2,1)} %get-tuple-element.26.refs_0_, bf16[3072,1024]{1,0:T(8,128)(2,1)} %get-tuple-element.27.refs_1_, bf16[1024,1024]{1,0:T(8,128)(2,1)} %get-tuple-element.28.refs_2_, ...), custom_call_target="tpu_custom_call" | custom-call | tf_op jit(solution)/shard_map/attn_tail/pallas_call | solution.py:575
  199.3 10.9 %update.1 = (bf16[1024,1024]{1,0:T(8,128)(2,1)}, bf16[1024,1024]{1,0:T(8,128)(2,1)}, f32[96,128]{1,0:T(8,128)}, f32[1,6,32,32]{3,2,1,0:T(8,128)}, f32[1,6,32,32]...) custom-call(bf16[1024,1024]{1,0:T(8,128)(2,1)} %get-tuple-element.25.out_h, ...), custom_call_target="tpu_custom_call" | custom-call | tf_op jit(solution)/shard_map/update/pallas_call | solution.py:625

commit v2 on v1

--- a/solution.py
+++ b/solution.py
@@ -190,8 +190,8 @@
     r=lax.rsqrt(jnp.mean(c*c,axis=-1,keepdims=True)+1e-12)
     return c*r,r
 
-PACE=[13, 15, 15, 30, 34, 34, 37, 37, 39, 42, 51, 53, 53, 53, 53, 58, 58, 58, 58, 60, 60, 60, 64, 64, 67, 70, 71, 73, 78, 78, 79, 84, 84, 84, 87, 90, 90, 92, 95, 99, 101, 103, 103, 103, 106, 106, 106, 108, 108, 108, 108, 108, 108, 108, 108, 108]
-OWN={1: 18, 2: 48, 3: 78}
+PACE=[13, 17, 17, 29, 31, 34, 37, 44, 44, 45, 45, 46, 46, 57, 58, 58, 58, 59, 61, 61, 61, 65, 70, 70, 70, 75, 75, 76, 78, 85, 85, 85, 85, 85, 88, 91, 91, 93, 97, 98, 101, 101, 103, 104, 106, 106, 106, 108, 108, 108, 108, 108, 108, 108, 108, 108]
+OWN={1: 17, 2: 44, 3: 70}
 
 def forward(mats,sources,cid,x,cot,bias,seg,pad,ndp,nfs):
     comm=bool(mats); n=len(mats); S=x.shape[0]//SEQ; T=x.shape[0]
@@ -497,16 +497,18 @@
             xs,xr=refs[o:o+2]; o+=2
             early=Reduce(*early_refs); late=Reduce(*late_refs); gl=late_refs[0]
         else: gl=gl_o
-        def p_load(i): return pltpu.make_async_copy(p_h.at[part(i,G)],pb.at[lax.rem(i,2)],psem.at[lax.rem(i,2)])
+        PB=3
+        def p_load(i): return [pltpu.make_async_copy(p_h.at[i*G+h],pb.at[lax.rem(i,PB),h],psem.at[lax.rem(i,PB),h]) for h in range(G)]
+        def begin_p(i):
+            for c in p_load(i): c.start()
         def chunk(i):
             out=[pltpu.make_async_copy(qkv_h.at[part(i+k*NI,R)],qkv_v.at[part(i+k*NI,R)],lsem.at[i,k]) for k in range(3)]
             return out+[pltpu.make_async_copy(a.at[part(i,R)],b.at[part(i,R)],lsem.at[i,3+k]) for k,(a,b) in enumerate(((d_h,d_v),(c_h,c_v)))]
-        p_load(jnp.int32(0)).start()
         def begin(i):
             for c in chunk(i): c.start()
-        loop(NI,begin)
-        wl=pltpu.make_async_copy(w_h,w_v,wsem.at[0]); wl.start()
-        dl=pltpu.make_async_copy(dp_h,dp_v,wsem.at[1]); dl.start()
+        begin(0); begin_p(0); begin(1); begin_p(1)
+        wl=[pltpu.make_async_copy(w_h.at[pl.ds(k*D,D)],w_v.at[pl.ds(k*D,D)],wsem.at[k]) for k in range(3)]
+        dl=pltpu.make_async_copy(dp_h,dp_v,wsem.at[3])
         ones_v[...]=jnp.ones_like(ones_v)
         if up:
             early.barrier()
@@ -519,11 +521,15 @@
                 states.append(pltpu.make_async_copy(a.at[0],st_v.at[k,x],xs.at[4+k]))
             for c in states: c.start()
         def back(i):
-            @pl.when(i<NI-1)
-            def _(): p_load(i+1).start()
-            for c in chunk(i): c.wait()
-            p_load(i).wait()
-            b=lax.rem(i,2)
+            @pl.when(i<NI-2)
+            def _(): begin(i+2); begin_p(i+2)
+            for k in range(3):
+                @pl.when(i==k+1)
+                def _(): wl[k].start()
+            @pl.when(i==4)
+            def _(): dl.start()
+            for c in chunk(i)+p_load(i): c.wait()
+            b=lax.rem(i,PB)
             for s in range(S):
                 cols=pl.ds(s*SEQ,SEQ)
                 for h in range(G):
@@ -543,7 +549,7 @@
                 def _(): early.middle()
         loop(NI,back)
         if up: late.start()
-        wl.wait(); dl.wait()
+        for c in wl+[dl]: c.wait()
         def finish(t):
             cols=part(t,RT)
             acc=dp_v[cols,:]
@@ -562,7 +568,7 @@
             early.finish(); late.finish()
         pltpu.make_async_copy(ig_v,ig_o,osem.at[0]).wait()
     V=pltpu.VMEM
-    scr=[V((2,G,S,SEQ,SEQ),BF),V((3*D,T),BF),V((D,T),BF),V((D,T),BF),V((T,D),F32),V((3*D,D),BF),V((T,D),BF),V((8,T),BF),DMA((2,)),DMA((NI,5)),DMA((2,)),DMA((1,))]
+    scr=[V((3,G,S,SEQ,SEQ),BF),V((3*D,T),BF),V((D,T),BF),V((D,T),BF),V((T,D),F32),V((3*D,D),BF),V((T,D),BF),V((8,T),BF),DMA((3,G)),DMA((NI,5)),DMA((4,)),DMA((1,))]
     ins=[p,qkvT,ctxT,dcT,dp1,wqkvT]; specs=[ANY]*6
     outs=[SDS((T,D),BF)]; ospecs=[ANY]
     if up:
@@ -579,10 +585,13 @@
     cap=state.shape[2]; NP=4
     def kernel(out_h,ig_h,g_in,st_v,b_in,own_s,out_o,ig_o,bg_o,mf_o,ms_o,bn_o,bl_o,m_st,v_st,v,sem):
         rows=out.shape[0]//NP
-        def moves(down):
-            return [pltpu.make_async_copy(*((v.at[k,pl.ds(i*rows,rows)],b.at[pl.ds(i*rows,rows)]) if down else (a.at[pl.ds(i*rows,rows)],v.at[k,pl.ds(i*rows,rows)])),sem.at[down,k,i])
-                for k,(a,b) in enumerate(((out_h,out_o),(ig_h,ig_o))) for i in range(NP)]
-        for c in moves(0): c.start()
+        def moves(down,k):
+            a,b=((out_h,out_o),(ig_h,ig_o))[k]
+            at=[pl.ds(i*rows,rows) for i in range(NP)]
+            if down: return [pltpu.make_async_copy(v.at[k,r],b.at[r],sem.at[1,k,i]) for i,r in enumerate(at)]
+            return [pltpu.make_async_copy(a.at[r],v.at[k,r],sem.at[0,k,i]) for i,r in enumerate(at)]
+        for k in range(2):
+            for c in moves(0,k): c.start()
         x=lax.axis_index("fsdp")
         owner=[own_s[b] for b in range(NB)]
         rank=[]
@@ -604,12 +613,14 @@
                 m_st[b]=m; v_st[b]=v
                 un=(m/(1.0-decay_first**STEP))/(jnp.sqrt(v/(1.0-decay_second**STEP))+adam_eps)
                 outs.append(dot_exact(dot_exact(left,un,1,0),right,1,1))
+                if j in (0,2):
+                    for c in moves(0,j//2): c.wait()
+                    for c in moves(1,j//2): c.start()
             back_=dot_exact(jnp.concatenate(outs,0),fold,1,1)*mask
             new=b_in[8*b0:8*(b0+n),:]-step_rate*dot_exact(sel,back_,0,0)
             bg_o[8*b0:8*(b0+n),:]=tiles
             bn_o[8*b0:8*(b0+n),:]=new
             bl_o[8*b0:8*(b0+n),:]=new.astype(BF)
-        for c,d in zip(moves(0),moves(1)): c.wait(); d.start()
         adam(0,NB,g_in[...])
         for c in range(mf_o.shape[1]):
             at=jnp.int32(0); hit=jnp.int32(0)
@@ -620,7 +631,8 @@
             filled=hit.astype(F32)
             mf_o[0,c]=m_st[at]*filled
             ms_o[0,c]=v_st[at]*filled
-        for c in moves(1): c.wait()
+        for k in range(2):
+            for c in moves(1,k): c.wait()
     m=SDS((1,cap,BS,BS),F32)
     return pl.pallas_call(kernel,
         out_shape=[SDS(out.shape,BF),SDS(ig.shape,BF),SDS((NB*8,128),F32),m,m,SDS((NB*8,128),F32),SDS((NB*8,128),BF)],

time: 211 us -> 203 us (0.962)
  Pallas kernels: 210 us -> 202 us
    pallas_call x1, Pallas kernels: 40.2 us -> 36.8 us  [attn_tail(): pl.pallas_call(kernel, out_shape=outs, in_specs=specs, out_specs=ospecs,...]
    pallas_call x1, Pallas kernels: 158 us -> 155 us  [forward(): pl.pallas_call(kernel, out_shape=[SDS((3 * D, T), BF), SDS((D, T), BF), S...]
where the time goes in v2:
time: 203 us
  Pallas kernels  202 us (100%)
    pallas_call x1, Pallas kernels, forward(): pl.pallas_call(kernel, out_shape=[SDS((3 * D, T), BF), SDS((D, T), BF), S...  155 us
    pallas_call x1, Pallas kernels, attn_tail(): pl.pallas_call(kernel, out_shape=outs, in_specs=specs, out_specs=ospecs,...  36.8 us
    pallas_call x1, Pallas kernels, update_step(): pl.pallas_call(kernel, out_shape=[SDS(out.shape, BF), SDS(ig.shape, BF),...  10 us

profile of v2, /device:TPU:0, one launch (start us, length us, event | category | flops | bytes accessed | tf_op | source)
XLA Modules:
  0.0 202.9 jit_solution(10053098340751325634)
XLA Ops:
  0.6 155.2 %forward.1 = (bf16[3072,1024]{1,0:T(8,128)(2,1)}, bf16[1024,1024]{1,0:T(8,128)(2,1)}, bf16[16,2,512,512]{3,2,1,0:T(8,128)(2,1)}, bf16[1024,1024]{1,0:T(8,128)(2,...) custom-call(bf16[1024,1024]{1,0:T(8,128)(2,1)} %bitcast.16, ...), custom_call_target="tpu_custom_call" | custom-call | tf_op jit(solution)/shard_map/forward/pallas_call | solution.py:408
  155.8 36.8 %attn_tail.1 = (bf16[1024,1024]{1,0:T(8,128)(2,1)}, f32[96,128]{1,0:T(8,128)}, f32[4,2,6,32,32]{4,3,2,1,0:T(8,128)}) custom-call(bf16[16,2,512,512]{3,2,1,0:T(8,128)(2,1)} %get-tuple-element.26.refs_0_, bf16[3072,1024]{1,0:T(8,128)(2,1)} %get-tuple-element.27.refs_1_, bf16[1024,1024]{1,0:T(8,128)(2,1)} %get-tuple-element.28.refs_2_, ...), custom_call_target="tpu_custom_call" | custom-call | tf_op jit(solution)/shard_map/attn_tail/pallas_call | solution.py:581
  192.7 10.0 %update.1 = (bf16[1024,1024]{1,0:T(8,128)(2,1)}, bf16[1024,1024]{1,0:T(8,128)(2,1)}, f32[96,128]{1,0:T(8,128)}, f32[1,6,32,32]{3,2,1,0:T(8,128)}, f32[1,6,32,32]...) custom-call(bf16[1024,1024]{1,0:T(8,128)(2,1)} %get-tuple-element.25.out_h, ...), custom_call_target="tpu_custom_call" | custom-call | tf_op jit(solution)/shard_map/update/pallas_call | solution.py:637

commit v3 on v2

--- a/solution.py
+++ b/solution.py
@@ -607,12 +607,13 @@
                 b=b0+j
                 at=jnp.minimum(rank[b],st_v.shape[2]-1)
                 first,second,left,right=[st_v[k,owner[b],at] for k in range(4)]
-                t=dot_exact(dot_exact(left,gs[j*BS:(j+1)*BS,:],0,0),right,1,0)
+                left,right=left.astype(BF),right.astype(BF)
+                t=nn(tn(left,gs[j*BS:(j+1)*BS,:].astype(BF)).astype(BF),right)
                 m=decay_first*first+(1.0-decay_first)*t
                 v=decay_second*second+(1.0-decay_second)*t*t
                 m_st[b]=m; v_st[b]=v
                 un=(m/(1.0-decay_first**STEP))/(jnp.sqrt(v/(1.0-decay_second**STEP))+adam_eps)
-                outs.append(dot_exact(dot_exact(left,un,1,0),right,1,1))
+                outs.append(nt(nn(left,un.astype(BF)).astype(BF),right))
                 if j in (0,2):
                     for c in moves(0,j//2): c.wait()
                     for c in moves(1,j//2): c.start()

time: 203 us -> 202 us (level)
  no operation moved by 1% of the time
where the time goes in v3:
time: 202 us
  Pallas kernels  201 us (100%)
    pallas_call x1, Pallas kernels, forward(): pl.pallas_call(kernel, out_shape=[SDS((3 * D, T), BF), SDS((D, T), BF), S...  155 us
    pallas_call x1, Pallas kernels, attn_tail(): pl.pallas_call(kernel, out_shape=outs, in_specs=specs, out_specs=ospecs,...  36.8 us
    pallas_call x1, Pallas kernels, update_step(): pl.pallas_call(kernel, out_shape=[SDS(out.shape, BF), SDS(ig.shape, BF),...  8.66 us

profile of v3, /device:TPU:0, one launch (start us, length us, event | category | flops | bytes accessed | tf_op | source)
XLA Modules:
  0.0 201.5 jit_solution(3724124248115700092)
XLA Ops:
  0.6 155.2 %forward.1 = (bf16[3072,1024]{1,0:T(8,128)(2,1)}, bf16[1024,1024]{1,0:T(8,128)(2,1)}, bf16[16,2,512,512]{3,2,1,0:T(8,128)(2,1)}, bf16[1024,1024]{1,0:T(8,128)(2,...) custom-call(bf16[1024,1024]{1,0:T(8,128)(2,1)} %bitcast.16, ...), custom_call_target="tpu_custom_call" | custom-call | tf_op jit(solution)/shard_map/forward/pallas_call | solution.py:408
  155.8 36.8 %attn_tail.1 = (bf16[1024,1024]{1,0:T(8,128)(2,1)}, f32[96,128]{1,0:T(8,128)}, f32[4,2,6,32,32]{4,3,2,1,0:T(8,128)}) custom-call(bf16[16,2,512,512]{3,2,1,0:T(8,128)(2,1)} %get-tuple-element.26.refs_0_, bf16[3072,1024]{1,0:T(8,128)(2,1)} %get-tuple-element.27.refs_1_, bf16[1024,1024]{1,0:T(8,128)(2,1)} %get-tuple-element.28.refs_2_, ...), custom_call_target="tpu_custom_call" | custom-call | tf_op jit(solution)/shard_map/attn_tail/pallas_call | solution.py:581
  192.7 8.7 %update.1 = (bf16[1024,1024]{1,0:T(8,128)(2,1)}, bf16[1024,1024]{1,0:T(8,128)(2,1)}, f32[96,128]{1,0:T(8,128)}, f32[1,6,32,32]{3,2,1,0:T(8,128)}, f32[1,6,32,32]...) custom-call(bf16[1024,1024]{1,0:T(8,128)(2,1)} %get-tuple-element.25.out_h, ...), custom_call_target="tpu_custom_call" | custom-call | tf_op jit(solution)/shard_map/update/pallas_call | solution.py:638

commit v4 on v3

--- a/solution.py
+++ b/solution.py
@@ -542,12 +542,13 @@
                     qkv_v[rv,cols]=nt(d,pr).astype(BF)
                     qkv_v[rk,cols]=(nt(q,ds)*0.125).astype(BF)
                     qkv_v[r,cols]=(nn(k,ds)*0.125).astype(BF)
-            gl[pl.ds(i,1),:]=nt(ones_v[...],qkv_v[part(i,R),:])[0:1,:]
-            gl[pl.ds(NI+i,1),:]=nt(ones_v[...],qkv_v[part(i+2*NI,R),:])[0:1,:]
             if up:
                 @pl.when(i==3)
                 def _(): early.middle()
         loop(NI,back)
+        for j,at in enumerate((0,2*D)):
+            sums=nt(ones_v[...],qkv_v[at:at+D,:])
+            for k in range(D//128): gl[j*(D//128)+k:j*(D//128)+k+1,:]=sums[0:1,k*128:(k+1)*128]
         if up: late.start()
         for c in wl+[dl]: c.wait()
         def finish(t):

time: 202 us -> 201 us (level)
  no operation moved by 1% of the time
where the time goes in v4:
time: 201 us
  Pallas kernels  200 us (100%)
    pallas_call x1, Pallas kernels, forward(): pl.pallas_call(kernel, out_shape=[SDS((3 * D, T), BF), SDS((D, T), BF), S...  155 us
    pallas_call x1, Pallas kernels, attn_tail(): pl.pallas_call(kernel, out_shape=outs, in_specs=specs, out_specs=ospecs,...  36.2 us
    pallas_call x1, Pallas kernels, update_step(): pl.pallas_call(kernel, out_shape=[SDS(out.shape, BF), SDS(ig.shape, BF),...  8.66 us

profile of v4, /device:TPU:0, one launch (start us, length us, event | category | flops | bytes accessed | tf_op | source)
XLA Modules:
  0.0 200.9 jit_solution(5355773684654787364)
XLA Ops:
  0.6 155.2 %forward.1 = (bf16[3072,1024]{1,0:T(8,128)(2,1)}, bf16[1024,1024]{1,0:T(8,128)(2,1)}, bf16[16,2,512,512]{3,2,1,0:T(8,128)(2,1)}, bf16[1024,1024]{1,0:T(8,128)(2,...) custom-call(bf16[1024,1024]{1,0:T(8,128)(2,1)} %bitcast.16, ...), custom_call_target="tpu_custom_call" | custom-call | tf_op jit(solution)/shard_map/forward/pallas_call | solution.py:408
  155.8 36.2 %attn_tail.1 = (bf16[1024,1024]{1,0:T(8,128)(2,1)}, f32[96,128]{1,0:T(8,128)}, f32[4,2,6,32,32]{4,3,2,1,0:T(8,128)}) custom-call(bf16[16,2,512,512]{3,2,1,0:T(8,128)(2,1)} %get-tuple-element.26.refs_0_, bf16[3072,1024]{1,0:T(8,128)(2,1)} %get-tuple-element.27.refs_1_, bf16[1024,1024]{1,0:T(8,128)(2,1)} %get-tuple-element.28.refs_2_, ...), custom_call_target="tpu_custom_call" | custom-call | tf_op jit(solution)/shard_map/attn_tail/pallas_call | solution.py:582
  192.0 8.7 %update.1 = (bf16[1024,1024]{1,0:T(8,128)(2,1)}, bf16[1024,1024]{1,0:T(8,128)(2,1)}, f32[96,128]{1,0:T(8,128)}, f32[1,6,32,32]{3,2,1,0:T(8,128)}, f32[1,6,32,32]...) custom-call(bf16[1024,1024]{1,0:T(8,128)(2,1)} %get-tuple-element.25.out_h, ...), custom_call_target="tpu_custom_call" | custom-call | tf_op jit(solution)/shard_map/update/pallas_call | solution.py:639
